TPU v7x, 256 devices: a whole 4x4x8 slice. The times are simulated.
256 devices in a mesh: dp: 16 (over x_lo, z), expert: 16 (over y, x_hi, core).
Axes of the slice: x: 4 (x_hi: 2, x_lo: 2; x = x_hi * 2 + x_lo), y: 4, z: 8, core: 2. Of those that a mesh axis runs over, the one named last changes fastest.
Arguments:
- query: bfloat16 [32768, 4096], P(('dp', 'expert')), may hold values from -6 to 6
- key: bfloat16 [32768, 4096], P(('dp', 'expert')), may hold values from -6 to 6
- value: bfloat16 [32768, 4096], P(('dp', 'expert')), may hold values from -6 to 6
- resid: bfloat16 [32768, 4096], P(('dp', 'expert')), may hold values from -6 to 6
- d_out: bfloat16 [32768, 4096], P(('dp', 'expert')), may hold values from -6 to 6
- routes: int32 [32768, 2], P(('dp', 'expert')), may hold values from 0 to 63, as said below
- gates: float32 [32768, 2], P(('dp', 'expert')), may hold values from 0.2 to 1
- w_up: bfloat16 [4096, 16384], P('dp', 'expert'), may hold values from -0.09375 to 0.09375
- w_down: bfloat16 [4096, 16384], P('dp', 'expert'), may hold values from -0.046875 to 0.046875
Outputs:
- grad_query: bfloat16 [32768, 4096], P(('dp', 'expert'))
- grad_key: bfloat16 [32768, 4096], P(('dp', 'expert'))
- grad_value: bfloat16 [32768, 4096], P(('dp', 'expert'))
- grad_up: bfloat16 [4096, 16384], P('dp', 'expert')
- grad_down: bfloat16 [4096, 16384], P('dp', 'expert')
Inputs may be any that keep to these rules, and one draw needn't show every extreme that they name: `routes`: the two experts of a token differ. Among the tokens of one device (aligned blocks of 128 rows) between 1 and 4 name expert 0, and some device has exactly 4.
All inputs are finite; a program needn't handle non-finite values.
Results may differ from a plain program's by a relative error of at most 0.011.
The roundings to bfloat16 on the way count: a program that leaves them out, or rounds other values in their place, can miss the bound.
Values may be sent and summed in bfloat16 or wider, within the bound.
A program may use at most 128 MiB of HBM per device.

v0:
```python
from functools import partial

import jax
import jax.numpy as jnp
from jax import lax
from jax.sharding import PartitionSpec as P

HEADS = 64
HEAD = 64
CAP = 4


EPS = 1e-06


def activate(hidden):
    outputs, pullback = jax.vjp(partial(jax.nn.gelu, approximate=True), hidden)
    return (outputs, pullback(jnp.ones_like(hidden))[0])


def attend_forward(query, key, value):
    length = query.shape[0]
    scaling = HEAD ** (-0.5)
    query_heads = query.reshape(length, HEADS, HEAD)
    key_heads = key.reshape(length, HEADS, HEAD)
    value_heads = value.reshape(length, HEADS, HEAD)
    scores = (
        jnp.einsum("shd,thd->hst", query_heads, key_heads, preferred_element_type=jnp.float32)
        * scaling
    )
    causal = jnp.arange(length)[:, None] >= jnp.arange(length)[None, :]
    scores = jnp.where(causal[None], scores, -jnp.inf)
    row_peak = jnp.max(scores, axis=-1, keepdims=True)
    weights = jnp.exp(scores - row_peak)
    probability = weights / jnp.sum(weights, axis=-1, keepdims=True)
    rounded = probability.astype(jnp.bfloat16)
    mixture = jnp.einsum("hst,thd->shd", rounded, value_heads, preferred_element_type=jnp.float32)
    return (probability, rounded, mixture.reshape(length, HEADS * HEAD))


def local(query, key, value, resid, d_out, routes, gates, w_up, w_down):
    tokens = query.shape[0]
    feature_count = query.shape[1]
    dp_count = lax.axis_size("dp")
    owner_count = lax.axis_size("expert")
    local_features = w_up.shape[0]
    local_units = w_up.shape[1]
    slot_count = CAP
    probability, rounded, mixture = attend_forward(query, key, value)
    state = resid.astype(jnp.float32) + mixture
    root_mean = jnp.sqrt(jnp.mean(state * state, axis=-1, keepdims=True) + EPS)
    normed = state / root_mean
    normed_input = normed.astype(jnp.bfloat16)
    upstream = d_out.astype(jnp.float32)
    chosen = routes == 0
    has_route = jnp.any(chosen, axis=1)
    picked_gate = jnp.sum(jnp.where(chosen, gates, jnp.zeros_like(gates)), axis=1)
    out_grad = (picked_gate[:, None] * upstream).astype(jnp.bfloat16)
    hit_count = has_route.astype(jnp.int32)
    slot_index = jnp.cumsum(hit_count) - 1
    slot_place = jnp.where(has_route, slot_index, slot_count)
    empty_rows = jnp.zeros((slot_count + 1, feature_count), jnp.bfloat16)
    send_input = empty_rows.at[slot_place].set(normed_input)[:slot_count]
    send_grad = empty_rows.at[slot_place].set(out_grad)[:slot_count]
    shared = (
        lax.all_gather(send_input, "expert", axis=0, tiled=True),
        lax.all_gather(send_grad, "expert", axis=0, tiled=True),
    )
    rows_input, rows_grad = (
        lax.all_to_all(shared[0], "dp", split_axis=1, concat_axis=0, tiled=True),
        lax.all_to_all(shared[1], "dp", split_axis=1, concat_axis=0, tiled=True),
    )
    row_total = rows_input.shape[0]
    first_term = jnp.dot(rows_input, w_up, preferred_element_type=jnp.float32)
    second_term = jnp.dot(rows_grad, w_down, preferred_element_type=jnp.float32)
    summed_pair = lax.psum(jnp.concatenate((first_term, second_term), axis=1), "dp")
    activation, gradient_slope = activate(summed_pair[:, :local_units])
    activation = activation.astype(jnp.bfloat16)
    hidden_grad = (summed_pair[:, local_units:] * gradient_slope).astype(jnp.bfloat16)
    grad_up = lax.dot_general(
        rows_input, hidden_grad, (((0,), (0,)), ((), ())), preferred_element_type=jnp.float32
    ).astype(jnp.bfloat16)
    grad_down = lax.dot_general(
        rows_grad, activation, (((0,), (0,)), ((), ())), preferred_element_type=jnp.float32
    ).astype(jnp.bfloat16)
    swapped = (
        hidden_grad.reshape(dp_count, owner_count, slot_count, local_units)
        .transpose(1, 0, 2, 3)
        .reshape(row_total, local_units)
    )
    own_share = lax.psum_scatter(
        lax.dot_general(
            swapped, w_up, (((1,), (1,)), ((), ())), preferred_element_type=jnp.float32
        ),
        "expert",
        scatter_dimension=0,
        tiled=True,
    )
    own_rounded = own_share.astype(jnp.bfloat16).reshape(dp_count, slot_count, local_features)
    home_rows = lax.all_to_all(own_rounded, "dp", split_axis=0, concat_axis=2, tiled=True).reshape(
        slot_count, feature_count
    )
    padded = jnp.concatenate([home_rows, jnp.zeros((1, feature_count), jnp.bfloat16)], axis=0)
    normed_grad = padded[slot_place].astype(jnp.float32)
    state_grad = (
        upstream
        + (normed_grad - normed * jnp.mean(normed_grad * normed, axis=-1, keepdims=True))
        / root_mean
    )
    state_grad = state_grad.astype(jnp.bfloat16)
    scaling = HEAD ** (-0.5)
    query_heads = query.reshape(tokens, HEADS, HEAD)
    key_heads = key.reshape(tokens, HEADS, HEAD)
    value_heads = value.reshape(tokens, HEADS, HEAD)
    grad_heads = state_grad.reshape(tokens, HEADS, HEAD)
    value_grad = jnp.einsum("hst,shd->thd", rounded, grad_heads, preferred_element_type=jnp.float32)
    prob_grad = jnp.einsum(
        "shd,thd->hst", grad_heads, value_heads, preferred_element_type=jnp.float32
    )
    row_delta = jnp.sum(
        grad_heads.astype(jnp.float32) * mixture.reshape(tokens, HEADS, HEAD), axis=-1
    ).T
    score_grad = (probability * (prob_grad - row_delta[:, :, None])).astype(jnp.bfloat16)
    query_grad = (
        jnp.einsum("hst,thd->shd", score_grad, key_heads, preferred_element_type=jnp.float32)
        * scaling
    )
    key_grad = (
        jnp.einsum("hst,shd->thd", score_grad, query_heads, preferred_element_type=jnp.float32)
        * scaling
    )
    shape_out = (tokens, feature_count)
    return (
        query_grad.reshape(shape_out).astype(jnp.bfloat16),
        key_grad.reshape(shape_out).astype(jnp.bfloat16),
        value_grad.reshape(shape_out).astype(jnp.bfloat16),
        grad_up,
        grad_down,
    )


def solution(mesh):
    in_specs = (
        P(("dp", "expert"), None),
        P(("dp", "expert"), None),
        P(("dp", "expert"), None),
        P(("dp", "expert"), None),
        P(("dp", "expert"), None),
        P(("dp", "expert"), None),
        P(("dp", "expert"), None),
        P("dp", "expert"),
        P("dp", "expert"),
    )
    out_specs = (
        P(("dp", "expert"), None),
        P(("dp", "expert"), None),
        P(("dp", "expert"), None),
        P("dp", "expert"),
        P("dp", "expert"),
    )
    return jax.shard_map(local, mesh=mesh, in_specs=in_specs, out_specs=out_specs, check_vma=False)
```

profile of v0, /device:TPU:2, one launch (start us, length us, event | category | flops | bytes accessed | tf_op | source)
XLA Modules:
  0.0 476.7 jit_solution(8189602463038572077)
XLA Ops:
  10.9 2.6 copy.72
  13.5 3.5 fusion.39
  17.0 2.9 fusion.19
  25.2 2.3 multiply_reduce_fusion
  32.3 25.8 %all-gather = bf16[16,4,4096]{2,1,0:T(4,128)(2,1)S(1)} all-gather(bf16[1,4,4096]{2,1,0:T(4,128)(2,1)S(1)} %slice_bitcast_fusion.1), channel_id=1, replica_groups=mesh['dp'=16,'expert'=16] {'expert'}, dimensions={0}, use_global_device_ids=true | all-gather | bytes 557056 | tf_op jit(solution)/shard_map/all_gather | solution.py:66
  61.3 9.9 %all-to-all-start = ((bf16[64,16,256]{2,0,1:T(8,128)(2,1)}), bf16[64,16,256]{2,0,1:T(8,128)(2,1)S(1)}, u32[]{:S(2)}, u32[]{:S(2)}) async-start(bf16[64,16,256]{2,0,1:T(8,128)(2,1)} %copy.75), calls=%async_computation | async-start | bytes 1048576 | tf_op jit(solution)/shard_map/all_to_all | solution.py:70
  71.3 2.7 scatter_custom_fusion.1
  73.9 25.1 %all-gather.1 = bf16[16,4,4096]{2,1,0:T(4,128)(2,1)} all-gather(bf16[1,4,4096]{2,1,0:T(4,128)(2,1)S(1)} %slice_bitcast_fusion), channel_id=1, replica_groups=mesh['dp'=16,'expert'=16] {'expert'}, dimensions={0}, use_global_device_ids=true | all-gather | bytes 557056 | tf_op jit(solution)/shard_map/all_gather | solution.py:67
  99.1 2.2 all_to_all.43
  103.3 6.4 %all-to-all-start.1 = ((bf16[64,16,256]{2,0,1:T(8,128)(2,1)}), bf16[64,16,256]{2,0,1:T(8,128)(2,1)}, u32[]{:S(2)}, u32[]{:S(2)}) async-start(bf16[64,16,256]{2,0,1:T(8,128)(2,1)} %copy.76), calls=%async_computation.1 | async-start | bytes 1048576 | tf_op jit(solution)/shard_map/all_to_all | solution.py:71
  109.9 2.7 fusion.40
  112.6 12.2 %all-to-all-done.1 = bf16[64,16,256]{2,0,1:T(8,128)(2,1)} async-done(((bf16[64,16,256]{2,0,1:T(8,128)(2,1)}), bf16[64,16,256]{2,0,1:T(8,128)(2,1)}, u32[]{:S(2)}, u32[]{:S(2)}) %all-to-all-start.1) | async-done | bytes 524320 | tf_op jit(solution)/shard_map/all_to_all | solution.py:71
  127.2 4.1 pad_maximum_fusion
  131.4 196.3 %all-reduce.3.cloned.1.call-done = f32[1024,2048]{0,1:T(8,128)} async-done(((f32[1024,2048]{0,1:T(8,128)}), f32[1024,2048]{0,1:T(8,128)}) %all-reduce.3.cloned.1.call-update) | async-done | bytes 8388624 | tf_op jit(solution)/shard_map/psum | solution.py:76
  327.7 5.9 %fusion.8 = bf16[1024,1024]{0,1:T(8,128)(2,1)} fusion(f32[1024,2048]{0,1:T(8,128)} %all-reduce.3.cloned.1.call-done), kind=kLoop, calls=%fused_computation.14 | loop fusion | flops 19922944 | bytes 10485760 | tf_op jit(solution)/shard_map/convert_element_type | solution.py:79
  333.6 3.9 copy.77
  337.5 4.1 reshape.116
  341.6 3.9 copy.78
  345.6 4.0 reshape.117
  349.6 3.3 fusion.42
  352.9 4.8 %fusion.21 = bf16[256,1024]{1,0:T(8,128)(2,1)} fusion(bf16[1024,256]{1,0:T(8,128)(2,1)} %bitcast.11, f32[1024,2048]{0,1:T(8,128)} %all-reduce.3.cloned.1.call-done), kind=kOutput, calls=%fused_computation.43 | convolution fusion | flops 546570240 | bytes 5242880 | tf_op jit(solution)/shard_map/dot_general | solution.py:83
  357.7 67.9 %reduce-scatter.2.cloned.1.call-done = f32[64,256]{1,0:T(8,128)} async-done(((f32[1024,256]{1,0:T(8,128)}), f32[64,256]{1,0:T(8,128)}) %reduce-scatter.2.cloned.1.call-update) | async-done | bytes 65552 | tf_op jit(solution)/shard_map/reduce_scatter | solution.py:91
  427.1 8.5 %all-to-all-start.2 = ((bf16[16,4,256]{2,1,0:T(4,128)(2,1)}), bf16[16,4,256]{2,1,0:T(4,128)(2,1)S(1)}, u32[]{:S(2)}, u32[]{:S(2)}) async-start(bf16[16,4,256]{2,1,0:T(4,128)(2,1)} %reshape.118), calls=%async_computation.3 | async-start | bytes 65536 | tf_op jit(solution)/shard_map/all_to_all | solution.py:100
  435.6 3.1 convolution_convert_fusion.1
  438.7 4.0 all-to-all-done.2
  446.5 3.1 fusion.11
  449.6 2.4 copy.79
  452.0 2.4 fusion.14
  454.5 4.1 convolution_convert_fusion
  459.8 2.5 multiply_convert_fusion.2
  464.0 2.4 copy.86
  466.3 2.3 copy.85
  (68 shorter events, 31.0 us)
Async XLA Ops:
  7.2 102.7 %copy-start = (bf16[256,1024]{1,0:T(8,128)(2,1)S(1)}, bf16[256,1024]{1,0:T(8,128)(2,1)}, u32[]{:S(2)}) copy-start(bf16[256,1024]{1,0:T(8,128)(2,1)} %param.16) | copy-start | bytes 1572868
  8.9 8.2 %copy-start.11 = (bf16[128,4096]{0,1:T(8,128)(2,1)}, bf16[128,4096]{0,1:T(8,128)(2,1)S(1)}, u32[]{:S(2)}) copy-start(bf16[128,4096]{0,1:T(8,128)(2,1)S(1)} %copy.68) | copy-start | bytes 3145732
  10.9 6.1 %copy-start.9 = (bf16[128,4096]{0,1:T(8,128)(2,1)}, bf16[128,4096]{0,1:T(8,128)(2,1)S(1)}, u32[]{:S(2)}) copy-start(bf16[128,4096]{0,1:T(8,128)(2,1)S(1)} %copy.69) | copy-start | bytes 3145732
  17.0 4.2 copy-start.6
  19.9 1.3 copy-start.2
  25.2 2.4 copy-start.4
  25.2 4.6 copy-start.14
  29.8 41.5 %copy-start.15 = (f32[128,2]{0,1:T(2,128)S(1)}, f32[128,2]{0,1:T(2,128)}, u32[]{:S(2)}) copy-start(f32[128,2]{0,1:T(2,128)} %param.15) | copy-start | bytes 3076
  61.3 42.0 %all-to-all-start = ((bf16[64,16,256]{2,0,1:T(8,128)(2,1)}), bf16[64,16,256]{2,0,1:T(8,128)(2,1)S(1)}, u32[]{:S(2)}, u32[]{:S(2)}) async-start(bf16[64,16,256]{2,0,1:T(8,128)(2,1)} %copy.75), calls=%async_computation | async-start | bytes 1048576 | tf_op jit(solution)/shard_map/all_to_all | solution.py:70
  103.3 21.5 %all-to-all-start.1 = ((bf16[64,16,256]{2,0,1:T(8,128)(2,1)}), bf16[64,16,256]{2,0,1:T(8,128)(2,1)}, u32[]{:S(2)}, u32[]{:S(2)}) async-start(bf16[64,16,256]{2,0,1:T(8,128)(2,1)} %copy.76), calls=%async_computation.1 | async-start | bytes 1048576 | tf_op jit(solution)/shard_map/all_to_all | solution.py:71
  109.7 218.0 %all-reduce.3.cloned.1.call-start = ((), (), s32[]{:S(2)}) async-start(), calls=%async_computation.4 | async-start | bytes 16777216 | tf_op jit(solution)/shard_map/psum | solution.py:76
  124.7 2.5 copy-start.1
  131.3 294.3 %reduce-scatter.2.cloned.1.call-start = ((), (), s32[]{:S(2)}) async-start(), calls=%async_computation.5 | async-start | bytes 1114112 | tf_op jit(solution)/shard_map/reduce_scatter | solution.py:91
  427.1 15.7 %all-to-all-start.2 = ((bf16[16,4,256]{2,1,0:T(4,128)(2,1)}), bf16[16,4,256]{2,1,0:T(4,128)(2,1)S(1)}, u32[]{:S(2)}, u32[]{:S(2)}) async-start(bf16[16,4,256]{2,1,0:T(4,128)(2,1)} %reshape.118), calls=%async_computation.3 | async-start | bytes 65536 | tf_op jit(solution)/shard_map/all_to_all | solution.py:100
  449.6 4.9 %copy-start.3 = (bf16[64,128,128]{1,2,0:T(8,128)(2,1)S(1)}, bf16[64,128,128]{1,2,0:T(8,128)(2,1)}, u32[]{:S(2)}) copy-start(bf16[64,128,128]{1,2,0:T(8,128)(2,1)} %copy-done.2) | copy-start | bytes 6291460
  452.0 6.5 %copy-start.5 = (bf16[128,4096]{0,1:T(8,128)(2,1)S(1)}, bf16[128,4096]{0,1:T(8,128)(2,1)}, u32[]{:S(2)}) copy-start(bf16[128,4096]{0,1:T(8,128)(2,1)} %copy.79) | copy-start | bytes 3145732
  452.0 6.5 %copy-start.7 = (bf16[128,4096]{0,1:T(8,128)(2,1)S(1)}, bf16[128,4096]{0,1:T(8,128)(2,1)}, u32[]{:S(2)}) copy-start(bf16[128,4096]{0,1:T(8,128)(2,1)} %copy.72) | copy-start | bytes 3145732
  452.0 6.5 %copy-start.8 = (f32[64,128,128]{1,2,0:T(8,128)S(1)}, f32[64,128,128]{1,2,0:T(8,128)}, u32[]{:S(2)}) copy-start(f32[64,128,128]{1,2,0:T(8,128)} %get-tuple-element.26) | copy-start | bytes 12582916
  458.5 1.2 copy-start.12
  459.8 2.5 copy-start.10
  464.0 4.6 copy-start.13
Sparse Core Ops, SparseCore 0:
  131.4 196.2 all-reduce.2
  353.0 72.5 reduce-scatter.1
where the time goes:
time: 479 us; the launch traced here: 477 us
  waiting for transfers between devices  280 us (58%)
  blocking collectives  51 us (11%)
  local copies, waits for them, and re-layouts  44.9 us (9%)
  matrix products  30.9 us (6%)
  other arithmetic  30.1 us (6%)
  starting transfers between devices  25.1 us (5%)
  between operations  14.3 us (3%)
    psum x1, waiting for transfers between devices, local(): lax.psum(jnp.concatenate((first_term, second_term), axis=1), 'dp')  196 us
    reduce_scatter x1, waiting for transfers between devices, local(): lax.psum_scatter(lax.dot_general(swapped, w_up, (((1,), (1,)), ((), ())),...  67.9 us
    all_gather x1, blocking collectives, local(): lax.all_gather(send_input, 'expert', axis=0, tiled=True)  25.8 us
    all_gather x1, blocking collectives, local(): lax.all_gather(send_grad, 'expert', axis=0, tiled=True)  25.1 us
    unnamed x40, local copies, waits for them, and re-layouts  14.2 us
    all_to_all x1, waiting for transfers between devices, local(): lax.all_to_all(shared[1], 'dp', split_axis=1, concat_axis=0, tiled=True)  12.2 us
    all_to_all x1, starting transfers between devices, local(): lax.all_to_all(shared[0], 'dp', split_axis=1, concat_axis=0, tiled=True)  9.94 us
  transfers between devices with their start and end apart: 5, of which 4 were waited for; matrix products, arithmetic and copies ran while one was open for 3% of the time, Pallas kernels for 0%

commit v1 on v0

v1 whole, which is shorter than its diff:
```python
import functools

import jax
import jax.numpy as jnp
from jax import lax
from jax.experimental import pallas as pl
from jax.experimental.pallas import tpu as pltpu
from jax.sharding import PartitionSpec as P

MESH = pl.DeviceIdType.MESH
F32 = jnp.float32
BF16 = jnp.bfloat16
D = 4096
SCALE = 0.125
EPS = 1e-06
Y_OFFSETS = (0, 1, 3, 2)
PAIRS = 32


def dot(a, b):
    return lax.dot_general(a, b, (((1,), (0,)), ((), ())), preferred_element_type=F32)


def dot_t(a, b):
    return lax.dot_general(a, b, (((1,), (1,)), ((), ())), preferred_element_type=F32)


def t_dot(a, b):
    return lax.dot_general(a, b, (((0,), (0,)), ((), ())), preferred_element_type=F32)


def iota(shape, dim):
    return lax.broadcasted_iota(jnp.int32, shape, dim)


def kernel(
    aux_ref, q_hbm, k_hbm, v_hbm, r_hbm, d_hbm, wu_hbm, wd_hbm,
    dq_hbm, dk_hbm, dv_hbm, gu_hbm, gd_hbm,
    q, k, v, r, d, wu, wd, keep, qr, dlo, state, prob,
    asend, arecv, g, part, rsp, rsm, ag, gu_acc, gd_acc, gu_out, gd_out,
    rsend, rcore, rysend, ryrecv, rxsend, rxrecv, hsend, hrecv,
    dq, dkb, dvb, dko, dvo,
    load_sem, out_sem, w_send, w_recv, a_send, a_recv, x_send, x_recv, c_send, c_recv, y_send, y_recv,
    rs_send, rs_recv, ag_send, ag_recv, rc_send, rc_recv, ry_send, ry_recv, rx_send, rx_recv, h_send, h_recv,
    o_send, o_recv,
):
    i = lax.axis_index("dp")
    j = lax.axis_index("expert")
    xl = i // 8
    z = i % 8
    y = j // 4
    xh = (j // 2) % 2
    c = j % 2
    x = xh * 2 + xl

    def dev(x_to, y_to, z_to, c_to):
        return ((x_to % 2) * 8 + z_to, y_to * 4 + (x_to // 2) * 2 + c_to)

    def z_peer(step):
        return dev(x, y, (z + step) % 8, c)

    def x_peer(step):
        return dev((x + step) % 4, y, z, c)

    def y_peer(step):
        return dev(x, (y + step) % 4, z, c)

    core_peer = dev(x, y, z, 1 - c)
    pair_peer = (((1 - xl) * 8 + z), j)

    barrier = pltpu.get_barrier_semaphore()
    peers = [z_peer(s) for s in range(1, 8)] + [x_peer(s) for s in range(1, 4)]
    peers += [y_peer(s) for s in range(1, 4)] + [core_peer]
    for peer in peers:
        pl.semaphore_signal(barrier, inc=1, device_id=peer, device_id_type=MESH)

    loads = []
    for n, (src, dst) in enumerate(((q_hbm, q), (k_hbm, k), (v_hbm, v), (r_hbm, r), (d_hbm, d))):
        loads.append(pltpu.make_async_copy(src, dst, load_sem.at[n]))
    own_cols = pl.ds(pl.multiple_of(xl * 512, 512), 512)
    other_cols = pl.ds(pl.multiple_of((1 - xl) * 512, 512), 512)
    loads.append(pltpu.make_async_copy(wd_hbm.at[:, own_cols], wd.at[xl], load_sem.at[5]))
    loads.append(pltpu.make_async_copy(wu_hbm.at[:, own_cols], wu.at[xl], load_sem.at[6]))
    for copy in loads:
        copy.start()

    pl.semaphore_wait(barrier, len(peers))

    sent = []

    def send(src, dst, send_sem, recv_sem, peer):
        copy = pltpu.make_async_remote_copy(
            src_ref=src, dst_ref=dst, send_sem=send_sem, recv_sem=recv_sem, device_id=peer, device_id_type=MESH
        )
        copy.start()
        sent.append(copy)

    def arrived(dst, send_sem, recv_sem, peer):
        pltpu.make_async_remote_copy(
            src_ref=dst, dst_ref=dst, send_sem=send_sem, recv_sem=recv_sem, device_id=peer, device_id_type=MESH
        ).wait_recv()

    send(wd_hbm.at[:, other_cols], wd.at[xl], w_send.at[0], w_recv.at[0], pair_peer)
    send(wu_hbm.at[:, other_cols], wu.at[xl], w_send.at[1], w_recv.at[1], pair_peer)

    flags = aux_ref[0:2, :]
    gate_row = aux_ref[2:3, :] * flags[0:1, :] + aux_ref[3:4, :] * flags[1:2, :]
    hit = jnp.maximum(flags[0:1, :], flags[1:2, :])
    upper = (iota((128, 128), 0) <= iota((128, 128), 1)).astype(BF16)
    hits = jnp.broadcast_to(hit, (8, 128))
    rank = dot(hits.astype(BF16), upper) - 1.0
    slot = iota((8, 128), 0).astype(F32)
    sel = jnp.where((rank == slot) & (slot < 4.0), hits, 0.0)
    sel_hi = jnp.where(rank == slot - 4.0, hits, 0.0)
    occupied = jnp.sum(sel, axis=1, keepdims=True)
    position = jnp.sum(sel * iota((8, 128), 1).astype(F32), axis=1, keepdims=True)
    gate_hi = jnp.sum(sel_hi * gate_row, axis=1, keepdims=True)
    sel_b = sel.astype(BF16)
    sel_both = jnp.concatenate([sel, sel_hi], axis=0).astype(BF16)
    keep[...] = (1.0 - t_dot(sel_b, jnp.ones((8, 128), BF16))).astype(BF16)
    seen = iota((8, 128), 1).astype(F32) <= position
    seen32 = jnp.concatenate([seen.astype(F32)] * 4, axis=0) > 0.5
    lane_head = iota((8, 256), 1) // 64

    def spread(rows):
        return jnp.concatenate([jnp.where(lane_head == h, rows, 0.0) for h in range(4)], axis=0).astype(BF16)

    def fold(rows):
        total = jnp.where(lane_head == 0, rows[0:8], 0.0)
        for h in range(1, 4):
            total = total + jnp.where(lane_head == h, rows[8 * h : 8 * h + 8], 0.0)
        return total

    for copy in loads[:5]:
        copy.wait()

    def routed_forward(n, squares):
        cols = pl.ds(pl.multiple_of(n * 256, 256), 256)
        q_rows = dot(sel_b, q[:, cols]) * SCALE
        qr[:, cols] = q_rows
        scores = jnp.where(seen32, dot_t(spread(q_rows), k[:, cols]), -jnp.inf)
        weights = jnp.exp(scores - jnp.max(scores, axis=1, keepdims=True))
        p = weights / jnp.sum(weights, axis=1, keepdims=True)
        prob[n] = p
        mixture = fold(dot(p.astype(BF16), v[:, cols]))
        st = dot(sel_b, r[:, cols]) + mixture
        state[:, cols] = st
        d_rows = dot(sel_both, d[:, cols])
        dlo[:, cols] = d_rows
        return squares + jnp.sum(st * st, axis=1, keepdims=True)

    squares = jnp.zeros((8, 1), F32)
    squares = lax.fori_loop(0, 16, routed_forward, squares, unroll=4)
    root_mean = jnp.sqrt(squares / D + EPS)
    low_row = iota((8, 256), 0) < 4

    def slot_rows(n):
        cols = slice(n * 256, n * 256 + 256)
        normed = state[:, cols] / root_mean * occupied
        return jnp.where(low_row, normed, gate_hi * dlo[8:16, cols])

    for n in range(8):
        asend[n] = jnp.concatenate([slot_rows(n), slot_rows(8 + n)], axis=0).astype(BF16)
    for s in range(1, 8):
        send(asend.at[(z + s) % 8], arecv.at[z], a_send.at[s - 1], a_recv.at[s - 1], z_peer(s))
    arecv[z] = asend[z]

    lane0 = iota((128, 128), 1) < 64
    causal = iota((256, 128), 0) % 128 >= iota((256, 128), 1)

    def two(rows):
        zero = jnp.zeros_like(rows)
        return jnp.concatenate([jnp.where(lane0, rows, zero), jnp.where(lane0, zero, rows)], axis=0)

    def attend(n, carry):
        cols = pl.ds(pl.multiple_of(n * 128, 128), 128)
        k2 = k[:, cols]
        qs = two(q[:, cols] * jnp.asarray(SCALE, BF16))
        scores = jnp.where(causal, dot_t(qs, k2), -jnp.inf)
        weights = jnp.exp(scores - jnp.max(scores, axis=1, keepdims=True))
        p = weights / jnp.sum(weights, axis=1, keepdims=True)
        pb = p.astype(BF16)
        ds = two(d[:, cols] * keep[...])
        dp = dot_t(ds, v[:, cols])
        delta = jnp.sum(pb.astype(F32) * dp, axis=1, keepdims=True)
        sg = (p * (dp - delta)).astype(BF16)
        dkb[:, cols] = t_dot(sg, qs)
        dvb[:, cols] = t_dot(pb, ds)
        sides = jnp.concatenate([sg[:128], sg[128:]], axis=1)
        dq[:, cols] = (dot(sides, two(k2)) * SCALE).astype(BF16)
        return carry

    done_pairs = [0]

    def attend_some(count):
        first = done_pairs[0]
        last = min(PAIRS, first + count)
        if last > first:
            lax.fori_loop(first, last, attend, 0)
        done_pairs[0] = last

    attend_some(4)

    for s in range(1, 8):
        arrived(arecv.at[(z + 8 - s) % 8], a_send.at[s - 1], a_recv.at[s - 1], z_peer(s))
    row = iota((128, 128), 0)
    col = iota((128, 128), 1)
    permute = ((row // 32 == (col // 4) % 4) & ((row % 32) // 4 == col // 16) & (row % 4 == col % 4)).astype(BF16)
    tiles = dot(permute, arecv[...].reshape(128, 256)).astype(BF16)
    g[y, c, x] = tiles.reshape(4, 32, 256)
    for s in range(1, 4):
        send(g.at[y, c, x], g.at[y, c, x], x_send.at[s - 1], x_recv.at[s - 1], x_peer(s))
    attend_some(2)
    for s in range(1, 4):
        arrived(g.at[y, c, (x + 4 - s) % 4], x_send.at[s - 1], x_recv.at[s - 1], x_peer(s))
    send(g.at[y, c], g.at[y, c], c_send.at[0], c_recv.at[0], core_peer)
    for w in range(1, 4):
        send(g.at[y, c], g.at[y, c], y_send.at[w - 1], y_recv.at[w - 1], y_peer(4 - Y_OFFSETS[w]))
    for copy in loads[5:]:
        copy.wait()
    arrived(wd.at[1 - xl], w_send.at[0], w_recv.at[0], pair_peer)
    arrived(wu.at[1 - xl], w_send.at[1], w_recv.at[1], pair_peer)

    def y_of(w):
        return (y + Y_OFFSETS[w]) % 4

    def rows_of(w, f, m):
        return g[y_of(w), :, :, f * 2 + m].reshape(256, 256)

    def gather(w):
        if w > 0:
            arrived(g.at[y_of(w), c], y_send.at[w - 1], y_recv.at[w - 1], y_peer(1))
            send(g.at[y_of(w), c], g.at[y_of(w), c], c_send.at[w], c_recv.at[w], core_peer)

    up_half = slice(0, 16)
    down_half = slice(16, 32)

    def reduce_start(w):
        arrived(g.at[y_of(w), 1 - c], c_send.at[w], c_recv.at[w], core_peer)
        hidden = dot(rows_of(w, 0, 0), wu[0]) + dot(rows_of(w, 1, 0), wu[1])
        part[w, :, :, 0:512] = hidden.astype(BF16).reshape(8, 32, 512)
        back = dot(rows_of(w, 0, 1), wd[0]) + dot(rows_of(w, 1, 1), wd[1])
        part[w, :, :, 512:1024] = back.astype(BF16).reshape(8, 32, 512)
        far = (z + 4) % 8
        send(part.at[w, far, up_half], rsp.at[w, 0, up_half], rs_send.at[w, 0], rs_recv.at[w, 0], z_peer(1))
        send(part.at[w, far, down_half], rsm.at[w, 0, down_half], rs_send.at[w, 4], rs_recv.at[w, 4], z_peer(7))

    def add(buf, w, s, rows, block):
        buf[w, s, rows] = (buf[w, s, rows].astype(F32) + part[w, block, rows].astype(F32)).astype(BF16)

    def reduce_step(w, s):
        up = (z + 4 - s) % 8
        down = (z + 4 + s) % 8
        if s == 1:
            arrived(rsp.at[w, 0, up_half], rs_send.at[w, 0], rs_recv.at[w, 0], z_peer(1))
            add(rsp, w, 0, up_half, up)
            rsp[w, 0, down_half] = part[w, up, down_half]
        else:
            arrived(rsp.at[w, s - 1], rs_send.at[w, s - 1], rs_recv.at[w, s - 1], z_peer(1))
            add(rsp, w, s - 1, slice(0, 32), up)
        send(rsp.at[w, s - 1], rsp.at[w, s], rs_send.at[w, s], rs_recv.at[w, s], z_peer(1))
        if s == 1:
            arrived(rsm.at[w, 0, down_half], rs_send.at[w, 4], rs_recv.at[w, 4], z_peer(7))
            add(rsm, w, 0, down_half, down)
            rsm[w, 0, up_half] = part[w, down, up_half]
        else:
            arrived(rsm.at[w, s - 1], rs_send.at[w, 3 + s], rs_recv.at[w, 3 + s], z_peer(7))
            add(rsm, w, s - 1, slice(0, 32), down)
        send(rsm.at[w, s - 1], rsm.at[w, s], rs_send.at[w, 4 + s], rs_recv.at[w, 4 + s], z_peer(7))

    def activate(w):
        arrived(rsp.at[w, 3], rs_send.at[w, 3], rs_recv.at[w, 3], z_peer(1))
        arrived(rsm.at[w, 3], rs_send.at[w, 7], rs_recv.at[w, 7], z_peer(7))
        total = part[w, z].astype(F32) + rsp[w, 3].astype(F32) + rsm[w, 3].astype(F32)
        h = total[:, 0:512]
        root = 0.7978845608028654
        inner = jnp.tanh(root * (h + 0.044715 * (h * h * h)))
        half = 0.5 * (1.0 + inner)
        slope = half + 0.5 * h * (1.0 - inner * inner) * (root * (1.0 + 3.0 * 0.044715 * (h * h)))
        ag[w, z, :, 0:512] = (total[:, 512:1024] * slope).astype(BF16)
        ag[w, z, :, 512:1024] = (h * half).astype(BF16)
        send(ag.at[w, z], ag.at[w, z], ag_send.at[w, 0], ag_recv.at[w, 0], z_peer(1))
        send(ag.at[w, z], ag.at[w, z], ag_send.at[w, 4], ag_recv.at[w, 4], z_peer(7))

    def forward(w, s):
        up = (z + 8 - s) % 8
        down = (z + s) % 8
        arrived(ag.at[w, up], ag_send.at[w, s - 1], ag_recv.at[w, s - 1], z_peer(1))
        rows = up_half if s == 3 else slice(0, 32)
        send(ag.at[w, up, rows], ag.at[w, up, rows], ag_send.at[w, s], ag_recv.at[w, s], z_peer(1))
        arrived(ag.at[w, down], ag_send.at[w, 3 + s], ag_recv.at[w, 3 + s], z_peer(7))
        rows = down_half if s == 3 else slice(0, 32)
        send(ag.at[w, down, rows], ag.at[w, down, rows], ag_send.at[w, 4 + s], ag_recv.at[w, 4 + s], z_peer(7))

    def gradients(w):
        far = (z + 4) % 8
        arrived(ag.at[w, far, up_half], ag_send.at[w, 3], ag_recv.at[w, 3], z_peer(1))
        arrived(ag.at[w, far, down_half], ag_send.at[w, 7], ag_recv.at[w, 7], z_peer(7))
        hidden_grad = ag[w, :, :, 0:512].reshape(256, 512)
        for f in range(2):
            back = dot_t(hidden_grad, wu[f]).astype(BF16)
            rsend[w, :, :, f * 256 : f * 256 + 256] = back.reshape(2, 128, 256)
        send(rsend.at[w, 1 - c], rcore.at[w], rc_send.at[w], rc_recv.at[w], core_peer)
        activation = ag[w, :, :, 512:1024].reshape(256, 512)
        for f in range(2):
            up = t_dot(rows_of(w, f, 0), hidden_grad)
            down = t_dot(rows_of(w, f, 1), activation)
            if w == 0:
                gu_acc[f] = up
                gd_acc[f] = down
            elif w < 3:
                gu_acc[f] += up
                gd_acc[f] += down
            else:
                gu_out[f] = (gu_acc[f] + up).astype(BF16)
                gd_out[f] = (gd_acc[f] + down).astype(BF16)

    def give_back(w):
        arrived(rcore.at[w], rc_send.at[w], rc_recv.at[w], core_peer)
        total = rsend[w, c].astype(F32) + rcore[w].astype(F32)
        rysend[w] = total.astype(BF16)
        if w > 0:
            send(rysend.at[w], ryrecv.at[w - 1], ry_send.at[w - 1], ry_recv.at[w - 1], y_peer(Y_OFFSETS[w]))

    stages = [
        lambda w: gather(w),
        lambda w: reduce_start(w),
        lambda w: reduce_step(w, 1),
        lambda w: reduce_step(w, 2),
        lambda w: reduce_step(w, 3),
        lambda w: activate(w),
        lambda w: forward(w, 1),
        lambda w: forward(w, 2),
        lambda w: forward(w, 3),
        lambda w: gradients(w),
        lambda w: give_back(w),
    ]
    spacing = 2
    for tick in range(len(stages) + 3 * spacing):
        for w in range(4):
            stage = tick - spacing * w
            if 0 <= stage < len(stages):
                stages[stage](w)
        attend_some(2)
    attend_some(PAIRS)

    send(gu_out.at[1 - xl], gu_hbm.at[:, own_cols], o_send.at[0], o_recv.at[0], pair_peer)
    send(gd_out.at[1 - xl], gd_hbm.at[:, own_cols], o_send.at[1], o_recv.at[1], pair_peer)
    outs = [
        pltpu.make_async_copy(gu_out.at[xl], gu_hbm.at[:, own_cols], out_sem.at[0]),
        pltpu.make_async_copy(gd_out.at[xl], gd_hbm.at[:, own_cols], out_sem.at[1]),
    ]
    for copy in outs:
        copy.start()

    total = rysend[0].astype(F32)
    for w in range(1, 4):
        arrived(ryrecv.at[w - 1], ry_send.at[w - 1], ry_recv.at[w - 1], y_peer(1))
        total = total + ryrecv[w - 1].astype(F32)
    rxsend[...] = total.astype(BF16).reshape(4, 32, 512)
    for s in range(1, 4):
        send(rxsend.at[(x + s) % 4], rxrecv.at[s - 1], rx_send.at[s - 1], rx_recv.at[s - 1], x_peer(s))
    returned = rxsend[x].astype(F32)
    for s in range(1, 4):
        arrived(rxrecv.at[s - 1], rx_send.at[s - 1], rx_recv.at[s - 1], x_peer(s))
        returned = returned + rxrecv[s - 1].astype(F32)
    returned = returned.astype(BF16)
    row32 = iota((128, 32), 0)
    col32 = iota((128, 32), 1)
    placed = (row32 // 16 == col32 // 4) & (row32 % 8 == col32 % 4)
    first = (placed & ((row32 // 8) % 2 == 0)).astype(BF16)
    second = (placed & ((row32 // 8) % 2 == 1)).astype(BF16)
    homes = dot(first, returned[:, 0:256]) + dot(second, returned[:, 256:512])
    hsend[...] = homes.astype(BF16).reshape(8, 16, 256)
    for s in range(1, 8):
        send(hsend.at[(z + s) % 8], hrecv.at[z], h_send.at[s - 1], h_recv.at[s - 1], z_peer(s))
    hrecv[z] = hsend[z]
    for s in range(1, 8):
        arrived(hrecv.at[(z + 8 - s) % 8], h_send.at[s - 1], h_recv.at[s - 1], z_peer(s))

    projection = jnp.zeros((8, 1), F32)
    for n in range(16):
        cols = slice(n * 256, n * 256 + 256)
        piece = hrecv[n % 8].astype(F32)[(n // 8) * 8 : (n // 8) * 8 + 8]
        projection = projection + jnp.sum(piece * (state[:, cols] / root_mean), axis=1, keepdims=True)
    projection = projection / D
    sel_t = t_dot(sel_b, (iota((8, 128), 0) == iota((8, 128), 1)).astype(BF16))[:, 0:8].astype(BF16)
    kept = keep[...]

    def routed_backward(n, carry):
        cols = pl.ds(pl.multiple_of(n * 256, 256), 256)
        tile = hrecv[n % 8].astype(F32)
        piece = jnp.where(n < 8, tile[0:8], tile[8:16])
        normed = state[:, cols] / root_mean
        grad = (dlo[0:8, cols] + (piece - normed * projection) / root_mean) * occupied
        gx = spread(grad)
        p = prob[n]
        pb = p.astype(BF16)
        dp = dot_t(gx, v[:, cols])
        delta = jnp.sum(pb.astype(F32) * dp, axis=1, keepdims=True)
        sg = (p * (dp - delta)).astype(BF16)
        q_grad = (fold(dot(sg, k[:, cols])) * SCALE).astype(BF16)
        dq[:, cols] = dq[:, cols] + dot(sel_t, q_grad).astype(BF16)
        dko[:, cols] = (dkb[:, cols] + t_dot(sg, spread(qr[:, cols]))).astype(BF16)
        dvo[:, cols] = (dvb[:, cols] + t_dot(pb, gx)).astype(BF16)
        return carry

    lax.fori_loop(0, 16, routed_backward, 0, unroll=2)
    for n, (src, dst) in enumerate(((dq, dq_hbm), (dko, dk_hbm), (dvo, dv_hbm))):
        copy = pltpu.make_async_copy(src, dst, out_sem.at[2 + n])
        copy.start()
        outs.append(copy)
    for copy in outs:
        copy.wait()
    arrived(gu_hbm.at[:, other_cols], o_send.at[0], o_recv.at[0], pair_peer)
    arrived(gd_hbm.at[:, other_cols], o_send.at[1], o_recv.at[1], pair_peer)
    for copy in sent:
        copy.wait_send()


def local(query, key, value, resid, d_out, routes, gates, w_up, w_down):
    aux = jnp.concatenate([(routes == 0).astype(F32), gates], axis=1).T
    hbm = pl.BlockSpec(memory_space=pl.ANY)
    rows = (128, D)
    vm = pltpu.VMEM
    dma = pltpu.SemaphoreType.DMA
    return pl.pallas_call(
        kernel,
        out_shape=(
            jax.ShapeDtypeStruct(rows, BF16),
            jax.ShapeDtypeStruct(rows, BF16),
            jax.ShapeDtypeStruct(rows, BF16),
            jax.ShapeDtypeStruct((256, 1024), BF16),
            jax.ShapeDtypeStruct((256, 1024), BF16),
        ),
        in_specs=[pl.BlockSpec(memory_space=pltpu.VMEM)] + [hbm] * 7,
        out_specs=(hbm,) * 5,
        scratch_shapes=[
            vm(rows, BF16), vm(rows, BF16), vm(rows, BF16), vm(rows, BF16), vm(rows, BF16),
            vm((2, 256, 512), BF16), vm((2, 256, 512), BF16), vm((128, 128), BF16),
            vm((8, D), F32), vm((16, D), F32), vm((8, D), F32), vm((16, 32, 128), F32),
            vm((8, 16, 256), BF16), vm((8, 16, 256), BF16), vm((4, 2, 4, 4, 32, 256), BF16),
            vm((4, 8, 32, 1024), BF16), vm((4, 4, 32, 1024), BF16), vm((4, 4, 32, 1024), BF16),
            vm((4, 8, 32, 1024), BF16),
            vm((2, 256, 512), F32), vm((2, 256, 512), F32), vm((2, 256, 512), BF16), vm((2, 256, 512), BF16),
            vm((4, 2, 128, 512), BF16), vm((4, 128, 512), BF16), vm((4, 128, 512), BF16), vm((3, 128, 512), BF16),
            vm((4, 32, 512), BF16), vm((3, 32, 512), BF16), vm((8, 16, 256), BF16), vm((8, 16, 256), BF16),
            vm(rows, BF16), vm(rows, F32), vm(rows, F32), vm(rows, BF16), vm(rows, BF16),
            dma((7,)), dma((5,)), dma((2,)), dma((2,)), dma((7,)), dma((7,)), dma((3,)), dma((3,)),
            dma((4,)), dma((4,)), dma((3,)), dma((3,)),
            dma((4, 8)), dma((4, 8)), dma((4, 8)), dma((4, 8)), dma((4,)), dma((4,)), dma((3,)), dma((3,)),
            dma((3,)), dma((3,)), dma((7,)), dma((7,)), dma((2,)), dma((2,)),
        ],
        compiler_params=pltpu.CompilerParams(
            collective_id=0, has_side_effects=True, vmem_limit_bytes=48 * 1024 * 1024
        ),
    )(aux, query, key, value, resid, d_out, w_up, w_down)


def solution(mesh):
    tokens = P(("dp", "expert"), None)
    weights = P("dp", "expert")
    return jax.shard_map(
        local,
        mesh=mesh,
        in_specs=(tokens,) * 7 + (weights,) * 2,
        out_specs=(tokens,) * 3 + (weights,) * 2,
        check_vma=False,
    )
```

time: 479 us -> 127 us (0.27)
  waiting for transfers between devices: 280 us -> 0 us
  Pallas kernels: 0 us -> 117 us
  blocking collectives: 51 us -> 0 us
  local copies, waits for them, and re-layouts: 44.9 us -> 6.58 us
  matrix products: 30.9 us -> 0 us
  other arithmetic: 30.1 us -> 0.7 us
  starting transfers between devices: 25.1 us -> 0 us
  between operations: 14.3 us -> 0.66 us
    psum x1 -> x0, waiting for transfers between devices: 196 us -> none  [local(): lax.psum(jnp.concatenate((first_term, second_term), axis=1), 'dp')]
    pallas_call x0 -> x1, Pallas kernels: none -> 117 us  [local(): pl.pallas_call(kernel, out_shape=(jax.ShapeDtypeStruct(rows, BF16), jax.S...]
    reduce_scatter x1 -> x0, waiting for transfers between devices: 67.9 us -> none  [local(): lax.psum_scatter(lax.dot_general(swapped, w_up, (((1,), (1,)), ((), ())),...]
    all_gather x2 -> x0, blocking collectives: 51 us -> none  [the longest x1 25.8 us: local(): lax.all_gather(send_input, 'expert', axis=0, tiled=True)]
    dot_general x10 -> x0, matrix products: 27.4 us -> none  [the longest x1 4.84 us: local(): lax.dot_general(rows_grad, activation, (((0,), (0,)), ((), ())), preferre...]
    all_to_all x3 -> x0, starting transfers between devices: 24.8 us -> none  [the longest x1 9.94 us: local(): lax.all_to_all(shared[0], 'dp', split_axis=1, concat_axis=0, tiled=True)]
    all_to_all x3 -> x0, waiting for transfers between devices: 16.2 us -> none  [the longest x1 12.2 us: local(): lax.all_to_all(shared[1], 'dp', split_axis=1, concat_axis=0, tiled=True)]
    convert_element_type x5 -> x1, other arithmetic: 12.7 us -> 0.69 us  [local(): aux = jnp.concatenate([(routes == 0).astype(F32), gates], axis=1).T]
  transfers between devices with their start and end apart: 5 -> 0, of which waited for: 4 -> 0; matrix products, arithmetic and copies ran while one was open for 3% -> 0% of each run, Pallas kernels for 0% -> 0%
where the time goes in v1:
time: 127 us; the launch traced here: 125 us
  Pallas kernels  117 us (92%)
  local copies, waits for them, and re-layouts  6.58 us (5%)
    pallas_call x1, Pallas kernels, local(): pl.pallas_call(kernel, out_shape=(jax.ShapeDtypeStruct(rows, BF16), jax.S...  117 us
    unnamed x11, local copies, waits for them, and re-layouts  6.58 us

profile of v1, /device:TPU:2, one launch (start us, length us, event | category | flops | bytes accessed | tf_op | source)
XLA Modules:
  0.0 125.2 jit_solution(4909472104114661369)
XLA Ops:
  0.6 0.0 copy-start.2
  0.6 0.7 compare_convert_fusion
  1.3 0.0 copy-done.2
  1.3 0.0 copy-start
  1.4 1.0 copy-done
  2.4 0.0 copy-start.1
  2.4 1.0 copy-done.1
  3.4 117.3 %shard_map.128 = (bf16[128,4096]{1,0:T(8,128)(2,1)S(1)}, bf16[128,4096]{1,0:T(8,128)(2,1)S(1)}, bf16[128,4096]{1,0:T(8,128)(2,1)S(1)}, bf16[256,1024]{1,0:T(8,128)(2,1)S(1)}, bf16[256,1024]{1,0:T(8,128)(2,1)S(1)}) custom-call(f32[4,128]{1,0:T(4,128)S(1)} %maximum_bitcast_fusion.aux_ref, bf16[128,4096]{1,0:T(8,128)(2,1)} %q_hbm.1, bf16[128,4096]{1,0:T(8,128)(2,1)} %k_hbm.1, ...), custom_call_target="tpu_custom_call" | custom-call | tf_op jit(solution)/shard_map/pallas_call | solution.py:427
  120.7 1.0 copy.19
  121.7 1.0 copy.20
  122.7 1.0 copy.21
  123.6 0.8 copy.22
  124.4 0.8 copy.23
  (1 shorter events, 0.0 us)
Async XLA Ops:
  0.6 0.7 copy-start.2
  1.3 1.0 copy-start
  2.4 1.0 copy-start.1

commit v2 on v1

v2 whole, which is shorter than its diff:
```python
import functools

import jax
import jax.numpy as jnp
from jax import lax
from jax.experimental import pallas as pl
from jax.experimental.pallas import tpu as pltpu
from jax.sharding import PartitionSpec as P

MESH = pl.DeviceIdType.MESH
F32 = jnp.float32
BF16 = jnp.bfloat16
D = 4096
SCALE = 0.125
EPS = 1e-06
Y_OFFSETS = (0, 1, 3, 2)
PAIRS = 32


def dot(a, b):
    return lax.dot_general(a, b, (((1,), (0,)), ((), ())), preferred_element_type=F32)


def dot_t(a, b):
    return lax.dot_general(a, b, (((1,), (1,)), ((), ())), preferred_element_type=F32)


def t_dot(a, b):
    return lax.dot_general(a, b, (((0,), (0,)), ((), ())), preferred_element_type=F32)


def iota(shape, dim):
    return lax.broadcasted_iota(jnp.int32, shape, dim)


def kernel(
    routes_ref, gates_ref, q_hbm, k_hbm, v_hbm, r_hbm, d_hbm, wu_hbm, wd_hbm,
    dq, dko, dvo, gu_hbm, gd_hbm,
    q, k, v, r, d, wu, wd, keep, qr, dlo, state, prob,
    asend, arecv, g, part, rs, ag, gu_acc, gd_acc, gu_out, gd_out,
    rsend, rcore, rysend, ryrecv, rxsend, rxrecv, hsend, hrecv,
    dkb, dvb,
    load_sem, out_sem, w_send, w_recv, a_send, a_recv, x_send, x_recv, c_send, c_recv, y_send, y_recv,
    rs_send, rs_recv, ag_send, ag_recv, rc_send, rc_recv, ry_send, ry_recv, rx_send, rx_recv, h_send, h_recv,
    o_send, o_recv,
):
    i = lax.axis_index("dp")
    j = lax.axis_index("expert")
    xl = i // 8
    z = i % 8
    y = j // 4
    xh = (j // 2) % 2
    c = j % 2
    x = xh * 2 + xl

    def dev(x_to, y_to, z_to, c_to):
        return ((x_to % 2) * 8 + z_to, y_to * 4 + (x_to // 2) * 2 + c_to)

    def z_peer(step):
        return dev(x, y, (z + step) % 8, c)

    def x_peer(step):
        return dev((x + step) % 4, y, z, c)

    def y_peer(step):
        return dev(x, (y + step) % 4, z, c)

    core_peer = dev(x, y, z, 1 - c)
    pair_peer = (((1 - xl) * 8 + z), j)

    barrier = pltpu.get_barrier_semaphore()
    peers = [z_peer(s) for s in range(1, 8)] + [x_peer(s) for s in range(1, 4)]
    peers += [y_peer(s) for s in range(1, 4)] + [core_peer]
    for peer in peers:
        pl.semaphore_signal(barrier, inc=1, device_id=peer, device_id_type=MESH)

    loads = []
    for n, (src, dst) in enumerate(((d_hbm, d), (q_hbm, q), (k_hbm, k), (r_hbm, r), (v_hbm, v))):
        loads.append(pltpu.make_async_copy(src, dst, load_sem.at[n]))
    own_cols = pl.ds(pl.multiple_of(xl * 512, 512), 512)
    other_cols = pl.ds(pl.multiple_of((1 - xl) * 512, 512), 512)
    loads.append(pltpu.make_async_copy(wd_hbm.at[:, own_cols], wd.at[xl], load_sem.at[5]))
    loads.append(pltpu.make_async_copy(wu_hbm.at[:, own_cols], wu.at[xl], load_sem.at[6]))
    for copy in loads:
        copy.start()

    sent = []

    def send(src, dst, send_sem, recv_sem, peer):
        copy = pltpu.make_async_remote_copy(
            src_ref=src, dst_ref=dst, send_sem=send_sem, recv_sem=recv_sem, device_id=peer, device_id_type=MESH
        )
        copy.start()
        sent.append(copy)

    def arrived(dst, send_sem, recv_sem, peer):
        pltpu.make_async_remote_copy(
            src_ref=dst, dst_ref=dst, send_sem=send_sem, recv_sem=recv_sem, device_id=peer, device_id_type=MESH
        ).wait_recv()

    flags = (routes_ref[...] == 0).astype(F32)
    picked = gates_ref[...] * flags
    gate_row = picked[0:1, :] + picked[1:2, :]
    hit = jnp.maximum(flags[0:1, :], flags[1:2, :])
    upper = (iota((128, 128), 0) <= iota((128, 128), 1)).astype(BF16)
    hits = jnp.broadcast_to(hit, (8, 128))
    rank = dot(hits.astype(BF16), upper) - 1.0
    slot = iota((8, 128), 0).astype(F32)
    sel = jnp.where((rank == slot) & (slot < 4.0), hits, 0.0)
    occupied = jnp.sum(sel, axis=1, keepdims=True)
    position = jnp.sum(sel * iota((8, 128), 1).astype(F32), axis=1, keepdims=True)
    gate = jnp.sum(sel * gate_row, axis=1, keepdims=True)
    sel_b = sel.astype(BF16)
    keep[...] = (1.0 - t_dot(sel_b, jnp.ones((8, 128), BF16))).astype(BF16)
    seen = iota((8, 128), 1).astype(F32) <= position
    seen32 = jnp.concatenate([seen] * 4, axis=0)
    lane_head = iota((8, 256), 1) // 64

    def spread(rows):
        return jnp.concatenate([jnp.where(lane_head == h, rows, 0.0) for h in range(4)], axis=0).astype(BF16)

    def fold(rows):
        total = jnp.where(lane_head == 0, rows[0:8], 0.0)
        for h in range(1, 4):
            total = total + jnp.where(lane_head == h, rows[8 * h : 8 * h + 8], 0.0)
        return total

    groups = [slice(n * 256, n * 256 + 256) for n in range(16)]
    loads[0].wait()
    for cols in groups:
        dlo[:, cols] = dot(sel_b, d[:, cols])
    for n in range(8):
        both = [gate * dlo[:, groups[n]], gate * dlo[:, groups[8 + n]]]
        asend[1, n] = jnp.concatenate(both, axis=0).astype(BF16)

    loads[1].wait()
    loads[2].wait()
    for cols in groups:
        qr[:, cols] = dot(sel_b, q[:, cols]) * SCALE
    scores = jnp.concatenate([dot_t(spread(qr[:, cols]), k[:, cols]) for cols in groups], axis=0)
    scores = jnp.where(jnp.concatenate([seen32] * 16, axis=0), scores, -jnp.inf)
    weights = jnp.exp(scores - jnp.max(scores, axis=1, keepdims=True))
    prob[...] = weights / jnp.sum(weights, axis=1, keepdims=True)

    pl.semaphore_wait(barrier, len(peers))

    def to_blocks(m):
        for s in range(1, 8):
            send(asend.at[m, (z + s) % 8], arecv.at[m, z], a_send.at[m, s - 1], a_recv.at[m, s - 1], z_peer(s))
        arecv[m, z] = asend[m, z]

    def send_weights(n):
        src, dst = ((wd_hbm, wd), (wu_hbm, wu))[n]
        for part_n in range(4):
            rows = slice(part_n * 64, part_n * 64 + 64)
            send(
                src.at[rows, other_cols], dst.at[xl, rows], w_send.at[n, part_n], w_recv.at[n, part_n], pair_peer
            )

    def weights_here(n):
        loads[5 + n].wait()
        dst = (wd, wu)[n]
        for part_n in range(4):
            rows = slice(part_n * 64, part_n * 64 + 64)
            arrived(dst.at[1 - xl, rows], w_send.at[n, part_n], w_recv.at[n, part_n], pair_peer)

    to_blocks(1)
    send_weights(0)

    loads[3].wait()
    loads[4].wait()
    for cols in groups:
        state[:, cols] = dot(sel_b, r[:, cols])
    squares = jnp.zeros((8, 256), F32)
    for n, cols in enumerate(groups):
        st = state[:, cols] + fold(dot(prob[n * 32 : n * 32 + 32, :].astype(BF16), v[:, cols]))
        state[:, cols] = st
        squares = squares + st * st
    squares = jnp.sum(squares, axis=1, keepdims=True)
    root_mean = jnp.sqrt(squares / D + EPS)
    for n in range(8):
        both = [state[:, groups[m]] / root_mean * occupied for m in (n, 8 + n)]
        asend[0, n] = jnp.concatenate(both, axis=0).astype(BF16)
    to_blocks(0)
    send_weights(1)

    lane0 = iota((128, 128), 1) < 64
    causal = iota((256, 128), 0) % 128 >= iota((256, 128), 1)

    def two(rows):
        zero = jnp.zeros_like(rows)
        return jnp.concatenate([jnp.where(lane0, rows, zero), jnp.where(lane0, zero, rows)], axis=0)

    def attend(n, carry):
        cols = pl.ds(pl.multiple_of(n * 128, 128), 128)
        k2 = k[:, cols]
        qs = two(q[:, cols] * jnp.asarray(SCALE, BF16))
        scores = jnp.where(causal, dot_t(qs, k2), -jnp.inf)
        weights = jnp.exp(scores - jnp.max(scores, axis=1, keepdims=True))
        p = weights / jnp.sum(weights, axis=1, keepdims=True)
        pb = p.astype(BF16)
        ds = two(d[:, cols] * keep[...])
        dp = dot_t(ds, v[:, cols])
        delta = jnp.sum(pb.astype(F32) * dp, axis=1, keepdims=True)
        sg = (p * (dp - delta)).astype(BF16)
        dkb[:, cols] = t_dot(sg, qs)
        dvb[:, cols] = t_dot(pb, ds)
        sides = jnp.concatenate([sg[:128], sg[128:]], axis=1)
        dq[:, cols] = (dot(sides, two(k2)) * SCALE).astype(BF16)
        return carry

    done_pairs = [0]

    def attend_some(count):
        first = done_pairs[0]
        last = min(PAIRS, first + count)
        if last > first:
            lax.fori_loop(first, last, attend, 0)
        done_pairs[0] = last

    row = iota((64, 128), 0)
    col = iota((64, 128), 1)
    permute = (row // 32 == (col // 8) % 2) & ((row % 32) // 4 == col // 16) & (row % 4 == col % 8)
    permute = permute.astype(BF16)

    def gather_x(m):
        for s in range(1, 8):
            arrived(arecv.at[m, (z + 8 - s) % 8], a_send.at[m, s - 1], a_recv.at[m, s - 1], z_peer(s))
        tiles = dot(permute, arecv[m].reshape(128, 256)).astype(BF16)
        block = g.at[m, y, c, x]
        block[...] = tiles.reshape(2, 32, 256)
        for s in range(1, 4):
            send(block, block, x_send.at[m, s - 1], x_recv.at[m, s - 1], x_peer(s))

    def gather_y(m):
        for s in range(1, 4):
            arrived(g.at[m, y, c, (x + 4 - s) % 4], x_send.at[m, s - 1], x_recv.at[m, s - 1], x_peer(s))
        block = g.at[m, y, c]
        send(block, block, c_send.at[m, 0], c_recv.at[m, 0], core_peer)
        send(block, block, y_send.at[m, 0], y_recv.at[m, 0], y_peer(3))
        send(block, block, y_send.at[m, 1], y_recv.at[m, 1], y_peer(1))

    def y_of(w):
        return (y + Y_OFFSETS[w]) % 4

    def rows_of(w, f, m):
        return g[m, y_of(w), :, :, f].reshape(256, 256)

    x_low = slice(0, 2)
    x_high = slice(2, 4)

    def gather(m, w):
        block = g.at[m, y_of(w), c]
        if w == 1:
            arrived(block, y_send.at[m, 0], y_recv.at[m, 0], y_peer(3))
            send(block.at[x_low], block.at[x_low], y_send.at[m, 2], y_recv.at[m, 2], y_peer(3))
        if w == 2:
            arrived(block, y_send.at[m, 1], y_recv.at[m, 1], y_peer(1))
            send(block.at[x_high], block.at[x_high], y_send.at[m, 3], y_recv.at[m, 3], y_peer(1))
        if w == 3:
            arrived(block.at[x_low], y_send.at[m, 2], y_recv.at[m, 2], y_peer(3))
            arrived(block.at[x_high], y_send.at[m, 3], y_recv.at[m, 3], y_peer(1))
        send(block, block, c_send.at[m, w], c_recv.at[m, w], core_peer)

    up_half = slice(0, 16)
    down_half = slice(16, 32)

    def reduce_start(m, w):
        arrived(g.at[m, y_of(w), 1 - c], c_send.at[m, w], c_recv.at[m, w], core_peer)
        right = (wu, wd)[m]
        terms = dot(rows_of(w, 0, m), right[0]) + dot(rows_of(w, 1, m), right[1])
        part[m, w] = terms.astype(BF16).reshape(8, 32, 512)
        far = part.at[m, w, (z + 4) % 8]
        ups, downs = rs.at[m, 0, w, 0], rs.at[m, 1, w, 0]
        send(far.at[up_half], ups.at[up_half], rs_send.at[m, 0, w, 0], rs_recv.at[m, 0, w, 0], z_peer(1))
        send(far.at[down_half], downs.at[down_half], rs_send.at[m, 1, w, 0], rs_recv.at[m, 1, w, 0], z_peer(7))

    def reduce_step(m, w, s):
        for side in range(2):
            block = (z + 4 - s) % 8 if side == 0 else (z + 4 + s) % 8
            here, fresh = (up_half, down_half) if side == 0 else (down_half, up_half)
            peer = z_peer(1) if side == 0 else z_peer(7)
            last = rs.at[m, side, w, s - 1]
            sems = rs_send.at[m, side, w, s - 1], rs_recv.at[m, side, w, s - 1]
            if s == 1:
                arrived(last.at[here], *sems, peer)
                last[here] = (last[here].astype(F32) + part[m, w, block, here].astype(F32)).astype(BF16)
                last[fresh] = part[m, w, block, fresh]
            else:
                arrived(last, *sems, peer)
                last[...] = (last[...].astype(F32) + part[m, w, block].astype(F32)).astype(BF16)
            send(last, rs.at[m, side, w, s], rs_send.at[m, side, w, s], rs_recv.at[m, side, w, s], peer)

    def reduced(m, w):
        total = part[m, w, z].astype(F32)
        for side in range(2):
            last = rs.at[m, side, w, 3]
            peer = z_peer(1) if side == 0 else z_peer(7)
            arrived(last, rs_send.at[m, side, w, 3], rs_recv.at[m, side, w, 3], peer)
            total = total + last[...].astype(F32)
        return total

    def activate(w):
        back = reduced(1, w)
        h = reduced(0, w)
        root = 0.7978845608028654
        inner = jnp.tanh(root * (h + 0.044715 * (h * h * h)))
        half = 0.5 * (1.0 + inner)
        slope = half + 0.5 * h * (1.0 - inner * inner) * (root * (1.0 + 3.0 * 0.044715 * (h * h)))
        ag[0, w, z] = (back * slope).astype(BF16)
        ag[1, w, z] = (h * half).astype(BF16)
        spread_out(0, w)

    def spread_out(m, w):
        send(ag.at[m, w, z], ag.at[m, w, z], ag_send.at[m, w, 0], ag_recv.at[m, w, 0], z_peer(1))
        send(ag.at[m, w, z], ag.at[m, w, z], ag_send.at[m, w, 4], ag_recv.at[m, w, 4], z_peer(7))

    def forward(m, w, s):
        up = (z + 8 - s) % 8
        down = (z + s) % 8
        block = ag.at[m, w, up]
        arrived(block, ag_send.at[m, w, s - 1], ag_recv.at[m, w, s - 1], z_peer(1))
        block = block.at[up_half] if s == 3 else block
        send(block, block, ag_send.at[m, w, s], ag_recv.at[m, w, s], z_peer(1))
        block = ag.at[m, w, down]
        arrived(block, ag_send.at[m, w, 3 + s], ag_recv.at[m, w, 3 + s], z_peer(7))
        block = block.at[down_half] if s == 3 else block
        send(block, block, ag_send.at[m, w, 4 + s], ag_recv.at[m, w, 4 + s], z_peer(7))

    def whole(m, w):
        far = (z + 4) % 8
        arrived(ag.at[m, w, far, up_half], ag_send.at[m, w, 3], ag_recv.at[m, w, 3], z_peer(1))
        arrived(ag.at[m, w, far, down_half], ag_send.at[m, w, 7], ag_recv.at[m, w, 7], z_peer(7))

    def input_gradient(w):
        whole(0, w)
        hidden_grad = ag[0, w].reshape(256, 512)
        for f in range(2):
            back = dot_t(hidden_grad, wu[f]).astype(BF16)
            rsend[w, :, :, f * 256 : f * 256 + 256] = back.reshape(2, 128, 256)
        send(rsend.at[w, 1 - c], rcore.at[w], rc_send.at[w], rc_recv.at[w], core_peer)

    def weight_gradient(m, w):
        acc, out = ((gu_acc, gu_out), (gd_acc, gd_out))[m]
        right = ag[m, w].reshape(256, 512)
        for f in range(2):
            term = t_dot(rows_of(w, f, m), right)
            if w == 0:
                acc[f] = term
            elif w < 3:
                acc[f] += term
            else:
                out[f] = (acc[f] + term).astype(BF16)

    def give_back(w):
        arrived(rcore.at[w], rc_send.at[w], rc_recv.at[w], core_peer)
        total = rsend[w, c].astype(F32) + rcore[w].astype(F32)
        rysend[w] = total.astype(BF16)
        if w > 0:
            send(rysend.at[w], ryrecv.at[w - 1], ry_send.at[w - 1], ry_recv.at[w - 1], y_peer(Y_OFFSETS[w]))

    def sum_y():
        total = rysend[0].astype(F32)
        for w in range(1, 4):
            arrived(ryrecv.at[w - 1], ry_send.at[w - 1], ry_recv.at[w - 1], y_peer(1))
            total = total + ryrecv[w - 1].astype(F32)
        rxsend[...] = total.astype(BF16).reshape(4, 32, 512)
        for s in range(1, 4):
            send(rxsend.at[(x + s) % 4], rxrecv.at[s - 1], rx_send.at[s - 1], rx_recv.at[s - 1], x_peer(s))

    def sum_x():
        returned = rxsend[x].astype(F32)
        for s in range(1, 4):
            arrived(rxrecv.at[s - 1], rx_send.at[s - 1], rx_recv.at[s - 1], x_peer(s))
            returned = returned + rxrecv[s - 1].astype(F32)
        returned = returned.astype(BF16)
        row32 = iota((128, 32), 0)
        col32 = iota((128, 32), 1)
        placed = (row32 // 16 == col32 // 4) & (row32 % 8 == col32 % 4)
        first = (placed & ((row32 // 8) % 2 == 0)).astype(BF16)
        second = (placed & ((row32 // 8) % 2 == 1)).astype(BF16)
        homes = dot(first, returned[:, 0:256]) + dot(second, returned[:, 256:512])
        hsend[...] = homes.astype(BF16).reshape(8, 16, 256)
        for s in range(1, 8):
            send(hsend.at[(z + s) % 8], hrecv.at[z], h_send.at[s - 1], h_recv.at[s - 1], z_peer(s))
        hrecv[z] = hsend[z]

    outs = []

    def hand_over(m):
        out, whole_out = ((gu_out, gu_hbm), (gd_out, gd_hbm))[m]
        send(out.at[1 - xl], whole_out.at[:, own_cols], o_send.at[m], o_recv.at[m], pair_peer)
        copy = pltpu.make_async_copy(out.at[xl], whole_out.at[:, own_cols], out_sem.at[m])
        copy.start()
        outs.append(copy)

    plan = [
        (attend_some, 2), (gather_x, 1), (attend_some, 7), (gather_y, 1), (gather_x, 0), (attend_some, 1),
        (weights_here, 0), (reduce_start, 1, 0), (attend_some, 4), (gather_y, 0), (reduce_step, 1, 0, 1),
        (gather, 1, 2), (gather, 1, 1), (weights_here, 1), (reduce_start, 0, 0), (reduce_start, 1, 2),
        (reduce_start, 1, 1), (reduce_step, 1, 0, 2), (attend_some, 1), (reduce_step, 0, 0, 1), (gather, 0, 2),
        (gather, 0, 1), (reduce_step, 1, 2, 1), (attend_some, 1), (reduce_step, 1, 1, 1), (gather, 1, 3),
        (reduce_start, 0, 1), (reduce_step, 1, 0, 3), (reduce_start, 1, 3), (reduce_step, 0, 0, 2),
        (gather, 0, 3), (reduce_step, 1, 2, 2), (reduce_start, 0, 2), (reduce_step, 1, 1, 2),
        (reduce_step, 0, 1, 1), (reduce_start, 0, 3), (reduce_step, 1, 3, 1), (reduce_step, 0, 0, 3),
        (attend_some, 1), (reduce_step, 1, 2, 3), (reduce_step, 0, 2, 1), (attend_some, 1),
        (reduce_step, 1, 1, 3), (attend_some, 1), (reduce_step, 0, 1, 2), (reduce_step, 0, 3, 1),
        (attend_some, 1), (reduce_step, 1, 3, 2), (attend_some, 1), (activate, 0), (attend_some, 2),
        (reduce_step, 0, 2, 2), (attend_some, 2), (reduce_step, 0, 1, 3), (attend_some, 1),
        (reduce_step, 0, 3, 2), (attend_some, 1), (reduce_step, 1, 3, 3), (attend_some, 1), (forward, 0, 0, 1),
        (attend_some, 1), (reduce_step, 0, 2, 3), (attend_some, 1), (activate, 1), (reduce_step, 0, 3, 3),
        (attend_some, 2), (forward, 0, 0, 2), (activate, 2), (forward, 0, 1, 1), (activate, 3),
        (forward, 0, 0, 3), (forward, 0, 2, 1), (forward, 0, 1, 2), (forward, 0, 3, 1), (input_gradient, 0),
        (weight_gradient, 0, 0), (give_back, 0), (forward, 0, 1, 3), (forward, 0, 2, 2), (forward, 0, 3, 2),
        (input_gradient, 1), (forward, 0, 2, 3), (weight_gradient, 0, 1), (give_back, 1), (forward, 0, 3, 3),
        (spread_out, 1, 0), (spread_out, 1, 1), (spread_out, 1, 2), (spread_out, 1, 3), (input_gradient, 2),
        (weight_gradient, 0, 2), (give_back, 2), (input_gradient, 3), (forward, 1, 0, 1), (forward, 1, 1, 1),
        (weight_gradient, 0, 3), (give_back, 3), (forward, 1, 2, 1), (forward, 1, 3, 1), (forward, 1, 0, 2),
        (forward, 1, 1, 2), (forward, 1, 2, 2), (forward, 1, 3, 2), (forward, 1, 0, 3), (sum_y,), (hand_over, 0),
        (forward, 1, 1, 3), (forward, 1, 2, 3), (forward, 1, 3, 3), (whole, 1, 0), (weight_gradient, 1, 0),
        (whole, 1, 1), (weight_gradient, 1, 1), (sum_x,), (whole, 1, 2), (weight_gradient, 1, 2), (whole, 1, 3),
        (weight_gradient, 1, 3), (hand_over, 1),
    ]
    for step, *which in plan:
        step(*which)
    attend_some(PAIRS)
    for s in range(1, 8):
        arrived(hrecv.at[(z + 8 - s) % 8], h_send.at[s - 1], h_recv.at[s - 1], z_peer(s))

    def piece(n):
        return hrecv[n % 8].astype(F32)[(n // 8) * 8 : (n // 8) * 8 + 8]

    inverse = 1.0 / root_mean
    projection = jnp.zeros((8, 256), F32)
    for n, cols in enumerate(groups):
        projection = projection + piece(n) * (state[:, cols] * inverse)
    projection = jnp.sum(projection, axis=1, keepdims=True) / D
    sel_t = t_dot(sel_b, (iota((8, 128), 0) == iota((8, 128), 1)).astype(BF16))[:, 0:8].astype(BF16)
    spreads = []
    for n, cols in enumerate(groups):
        normed = state[:, cols] * inverse
        grad = (dlo[:, cols] + (piece(n) - normed * projection) * inverse) * occupied
        spreads.append(spread(grad))
    p = prob[...]
    pb = p.astype(BF16)
    dp = jnp.concatenate([dot_t(spreads[n], v[:, cols]) for n, cols in enumerate(groups)], axis=0)
    delta = jnp.sum(pb.astype(F32) * dp, axis=1, keepdims=True)
    sg = (p * (dp - delta)).astype(BF16)
    for n, cols in enumerate(groups):
        mine = slice(n * 32, n * 32 + 32)
        q_grad = (fold(dot(sg[mine], k[:, cols])) * SCALE).astype(BF16)
        dq[:, cols] = dq[:, cols] + dot(sel_t, q_grad).astype(BF16)
        dko[:, cols] = (dkb[:, cols] + t_dot(sg[mine], spread(qr[:, cols]))).astype(BF16)
        dvo[:, cols] = (dvb[:, cols] + t_dot(pb[mine], spreads[n])).astype(BF16)

    for copy in outs:
        copy.wait()
    arrived(gu_hbm.at[:, other_cols], o_send.at[0], o_recv.at[0], pair_peer)
    arrived(gd_hbm.at[:, other_cols], o_send.at[1], o_recv.at[1], pair_peer)
    for copy in sent:
        copy.wait_send()


def write_out(*refs):
    sems = refs[10]
    copies = [pltpu.make_async_copy(refs[n], refs[5 + n], sems.at[n]) for n in range(5)]
    for copy in copies:
        copy.start()
    for copy in copies:
        copy.wait()


def local(query, key, value, resid, d_out, routes, gates, w_up, w_down):
    hbm = pl.BlockSpec(memory_space=pl.ANY)
    pinned = pl.BlockSpec(memory_space=pltpu.HBM)
    vmem = pl.BlockSpec(memory_space=pltpu.VMEM)
    rows = (128, D)
    vm = pltpu.VMEM
    dma = pltpu.SemaphoreType.DMA
    results = pl.pallas_call(
        kernel,
        out_shape=(
            jax.ShapeDtypeStruct(rows, BF16),
            jax.ShapeDtypeStruct(rows, BF16),
            jax.ShapeDtypeStruct(rows, BF16),
            jax.ShapeDtypeStruct((256, 1024), BF16),
            jax.ShapeDtypeStruct((256, 1024), BF16),
        ),
        in_specs=[vmem, vmem] + [hbm] * 5 + [pinned] * 2,
        out_specs=(vmem,) * 3 + (hbm,) * 2,
        scratch_shapes=[
            vm(rows, BF16), vm(rows, BF16), vm(rows, BF16), vm(rows, BF16), vm(rows, BF16),
            vm((2, 256, 512), BF16), vm((2, 256, 512), BF16), vm((128, 128), BF16),
            vm((8, D), F32), vm((8, D), F32), vm((8, D), F32), vm((512, 128), F32),
            vm((2, 8, 16, 256), BF16), vm((2, 8, 16, 256), BF16), vm((2, 4, 2, 4, 2, 32, 256), BF16),
            vm((2, 4, 8, 32, 512), BF16), vm((2, 2, 4, 4, 32, 512), BF16),
            vm((2, 4, 8, 32, 512), BF16),
            vm((2, 256, 512), F32), vm((2, 256, 512), F32), vm((2, 256, 512), BF16), vm((2, 256, 512), BF16),
            vm((4, 2, 128, 512), BF16), vm((4, 128, 512), BF16), vm((4, 128, 512), BF16), vm((3, 128, 512), BF16),
            vm((4, 32, 512), BF16), vm((3, 32, 512), BF16), vm((8, 16, 256), BF16), vm((8, 16, 256), BF16),
            vm(rows, F32), vm(rows, F32),
            dma((7,)), dma((2,)), dma((2, 4)), dma((2, 4)), dma((2, 7)), dma((2, 7)), dma((2, 3)), dma((2, 3)),
            dma((2, 4)), dma((2, 4)), dma((2, 4)), dma((2, 4)),
            dma((2, 2, 4, 4)), dma((2, 2, 4, 4)), dma((2, 4, 8)), dma((2, 4, 8)), dma((4,)), dma((4,)), dma((3,)), dma((3,)),
            dma((3,)), dma((3,)), dma((7,)), dma((7,)), dma((2,)), dma((2,)),
        ],
        compiler_params=pltpu.CompilerParams(
            collective_id=0, has_side_effects=True, vmem_limit_bytes=61180000
        ),
    )(routes.T, gates.T, query, key, value, resid, d_out, w_up, w_down)
    return pl.pallas_call(
        write_out,
        out_shape=tuple(jax.ShapeDtypeStruct(part.shape, part.dtype) for part in results),
        in_specs=[vmem] * 5,
        out_specs=(hbm,) * 5,
        scratch_shapes=[dma((5,))],
    )(*results)


def solution(mesh):
    tokens = P(("dp", "expert"), None)
    weights = P("dp", "expert")
    return jax.shard_map(
        local,
        mesh=mesh,
        in_specs=(tokens,) * 7 + (weights,) * 2,
        out_specs=(tokens,) * 3 + (weights,) * 2,
        check_vma=False,
    )
```

time: 127 us -> 103 us (0.81); the launches traced: 125 us -> 103 us
  Pallas kernels: 117 us -> 102 us
  local copies, waits for them, and re-layouts: 6.58 us -> 0 us
    pallas_call x1, Pallas kernels: 117 us -> 97.7 us  [local(): pl.pallas_call(kernel, out_shape=(jax.ShapeDtypeStruct(rows, BF16), jax.S...]
    unnamed x11 -> x0, local copies, waits for them, and re-layouts: 6.58 us -> none
    pallas_call x0 -> x1, Pallas kernels: none -> 4.19 us  [local(): pl.pallas_call(write_out, out_shape=tuple((jax.ShapeDtypeStruct(part.shap...]
where the time goes in v2:
time: 103 us
  Pallas kernels  102 us (99%)
    pallas_call x1, Pallas kernels, local(): pl.pallas_call(kernel, out_shape=(jax.ShapeDtypeStruct(rows, BF16), jax.S...  97.7 us
    pallas_call x1, Pallas kernels, local(): pl.pallas_call(write_out, out_shape=tuple((jax.ShapeDtypeStruct(part.shap...  4.19 us

profile of v2, /device:TPU:2, one launch (start us, length us, event | category | flops | bytes accessed | tf_op | source)
XLA Modules:
  0.0 102.7 jit_solution(382855382403698173)
XLA Ops:
  0.6 97.7 %shard_map.128 = (bf16[128,4096]{1,0:T(8,128)(2,1)}, bf16[128,4096]{1,0:T(8,128)(2,1)}, bf16[128,4096]{1,0:T(8,128)(2,1)}, bf16[256,1024]{1,0:T(8,128)(2,1)}, bf16[256,1024]{1,0:T(8,128)(2,1)}) custom-call(s32[2,128]{1,0:T(2,128)} %bitcast.2, f32[2,128]{1,0:T(2,128)} %bitcast.3, bf16[128,4096]{1,0:T(8,128)(2,1)} %q_hbm.1, bf16[128,4096]{1,0:T(8,128)(2,1)} %k_hbm.1, ...), custom_call_target="tpu_custom_call" | custom-call | tf_op jit(solution)/shard_map/pallas_call | solution.py:480
  98.4 4.2 %shard_map.129 = (bf16[128,4096]{1,0:T(8,128)(2,1)}, bf16[128,4096]{1,0:T(8,128)(2,1)}, bf16[128,4096]{1,0:T(8,128)(2,1)}, bf16[256,1024]{1,0:T(8,128)(2,1)}, bf16[256,1024]{1,0:T(8,128)(2,1)}) custom-call(bf16[128,4096]{1,0:T(8,128)(2,1)} %get-tuple-element.10.refs_0_, bf16[128,4096]{1,0:T(8,128)(2,1)} %get-tuple-element.11.refs_1_, ...), custom_call_target="tpu_custom_call" | custom-call | tf_op jit(solution)/shard_map/pallas_call | solution.py:511

commit v3 on v2

--- a/solution.py
+++ b/solution.py
@@ -36,7 +36,7 @@
 def kernel(
     routes_ref, gates_ref, q_hbm, k_hbm, v_hbm, r_hbm, d_hbm, wu_hbm, wd_hbm,
     dq, dko, dvo, gu_hbm, gd_hbm,
-    q, k, v, r, d, wu, wd, keep, qr, dlo, state, prob,
+    q, k, v, r, d, wu, wd, wx, keep, qr, dlo, state, prob,
     asend, arecv, g, part, rs, ag, gu_acc, gd_acc, gu_out, gd_out,
     rsend, rcore, rysend, ryrecv, rxsend, rxrecv, hsend, hrecv,
     dkb, dvb,
@@ -81,6 +81,8 @@
     other_cols = pl.ds(pl.multiple_of((1 - xl) * 512, 512), 512)
     loads.append(pltpu.make_async_copy(wd_hbm.at[:, own_cols], wd.at[xl], load_sem.at[5]))
     loads.append(pltpu.make_async_copy(wu_hbm.at[:, own_cols], wu.at[xl], load_sem.at[6]))
+    loads.append(pltpu.make_async_copy(wd_hbm.at[:, other_cols], wx.at[0], load_sem.at[7]))
+    loads.append(pltpu.make_async_copy(wu_hbm.at[:, other_cols], wx.at[1], load_sem.at[8]))
     for copy in loads:
         copy.start()
 
@@ -150,11 +152,12 @@
         arecv[m, z] = asend[m, z]
 
     def send_weights(n):
-        src, dst = ((wd_hbm, wd), (wu_hbm, wu))[n]
+        dst = (wd, wu)[n]
+        loads[7 + n].wait()
         for part_n in range(4):
             rows = slice(part_n * 64, part_n * 64 + 64)
             send(
-                src.at[rows, other_cols], dst.at[xl, rows], w_send.at[n, part_n], w_recv.at[n, part_n], pair_peer
+                wx.at[n, rows], dst.at[xl, rows], w_send.at[n, part_n], w_recv.at[n, part_n], pair_peer
             )
 
     def weights_here(n):
@@ -164,8 +167,8 @@
             rows = slice(part_n * 64, part_n * 64 + 64)
             arrived(dst.at[1 - xl, rows], w_send.at[n, part_n], w_recv.at[n, part_n], pair_peer)
 
+    send_weights(0)
     to_blocks(1)
-    send_weights(0)
 
     loads[3].wait()
     loads[4].wait()
@@ -182,7 +185,6 @@
         both = [state[:, groups[m]] / root_mean * occupied for m in (n, 8 + n)]
         asend[0, n] = jnp.concatenate(both, axis=0).astype(BF16)
     to_blocks(0)
-    send_weights(1)
 
     lane0 = iota((128, 128), 1) < 64
     causal = iota((256, 128), 0) % 128 >= iota((256, 128), 1)
@@ -395,31 +397,31 @@
         outs.append(copy)
 
     plan = [
-        (attend_some, 2), (gather_x, 1), (attend_some, 7), (gather_y, 1), (gather_x, 0), (attend_some, 1),
-        (weights_here, 0), (reduce_start, 1, 0), (attend_some, 4), (gather_y, 0), (reduce_step, 1, 0, 1),
-        (gather, 1, 2), (gather, 1, 1), (weights_here, 1), (reduce_start, 0, 0), (reduce_start, 1, 2),
-        (reduce_start, 1, 1), (reduce_step, 1, 0, 2), (attend_some, 1), (reduce_step, 0, 0, 1), (gather, 0, 2),
-        (gather, 0, 1), (reduce_step, 1, 2, 1), (attend_some, 1), (reduce_step, 1, 1, 1), (gather, 1, 3),
-        (reduce_start, 0, 1), (reduce_step, 1, 0, 3), (reduce_start, 1, 3), (reduce_step, 0, 0, 2),
-        (gather, 0, 3), (reduce_step, 1, 2, 2), (reduce_start, 0, 2), (reduce_step, 1, 1, 2),
-        (reduce_step, 0, 1, 1), (reduce_start, 0, 3), (reduce_step, 1, 3, 1), (reduce_step, 0, 0, 3),
-        (attend_some, 1), (reduce_step, 1, 2, 3), (reduce_step, 0, 2, 1), (attend_some, 1),
-        (reduce_step, 1, 1, 3), (attend_some, 1), (reduce_step, 0, 1, 2), (reduce_step, 0, 3, 1),
-        (attend_some, 1), (reduce_step, 1, 3, 2), (attend_some, 1), (activate, 0), (attend_some, 2),
-        (reduce_step, 0, 2, 2), (attend_some, 2), (reduce_step, 0, 1, 3), (attend_some, 1),
-        (reduce_step, 0, 3, 2), (attend_some, 1), (reduce_step, 1, 3, 3), (attend_some, 1), (forward, 0, 0, 1),
-        (attend_some, 1), (reduce_step, 0, 2, 3), (attend_some, 1), (activate, 1), (reduce_step, 0, 3, 3),
-        (attend_some, 2), (forward, 0, 0, 2), (activate, 2), (forward, 0, 1, 1), (activate, 3),
-        (forward, 0, 0, 3), (forward, 0, 2, 1), (forward, 0, 1, 2), (forward, 0, 3, 1), (input_gradient, 0),
-        (weight_gradient, 0, 0), (give_back, 0), (forward, 0, 1, 3), (forward, 0, 2, 2), (forward, 0, 3, 2),
-        (input_gradient, 1), (forward, 0, 2, 3), (weight_gradient, 0, 1), (give_back, 1), (forward, 0, 3, 3),
-        (spread_out, 1, 0), (spread_out, 1, 1), (spread_out, 1, 2), (spread_out, 1, 3), (input_gradient, 2),
-        (weight_gradient, 0, 2), (give_back, 2), (input_gradient, 3), (forward, 1, 0, 1), (forward, 1, 1, 1),
-        (weight_gradient, 0, 3), (give_back, 3), (forward, 1, 2, 1), (forward, 1, 3, 1), (forward, 1, 0, 2),
-        (forward, 1, 1, 2), (forward, 1, 2, 2), (forward, 1, 3, 2), (forward, 1, 0, 3), (sum_y,), (hand_over, 0),
-        (forward, 1, 1, 3), (forward, 1, 2, 3), (forward, 1, 3, 3), (whole, 1, 0), (weight_gradient, 1, 0),
-        (whole, 1, 1), (weight_gradient, 1, 1), (sum_x,), (whole, 1, 2), (weight_gradient, 1, 2), (whole, 1, 3),
-        (weight_gradient, 1, 3), (hand_over, 1),
+        (attend_some, 2), (gather_x, 1), (attend_some, 4), (gather_x, 0), (send_weights, 1), (gather_y, 1),
+        (attend_some, 1), (weights_here, 0), (reduce_start, 1, 0), (attend_some, 2), (gather_y, 0),
+        (gather, 1, 1), (gather, 1, 2), (reduce_start, 1, 1), (reduce_start, 1, 2), (weights_here, 1),
+        (reduce_start, 0, 0), (reduce_step, 1, 0, 1), (gather, 1, 3), (gather, 0, 1), (gather, 0, 2),
+        (reduce_start, 1, 3), (reduce_start, 0, 1), (reduce_start, 0, 2), (reduce_step, 1, 1, 1),
+        (reduce_step, 1, 2, 1), (reduce_step, 0, 0, 1), (gather, 0, 3), (reduce_step, 1, 0, 2),
+        (reduce_start, 0, 3), (reduce_step, 1, 3, 1), (reduce_step, 0, 1, 1), (reduce_step, 0, 2, 1),
+        (attend_some, 1), (reduce_step, 1, 1, 2), (reduce_step, 1, 2, 2), (reduce_step, 0, 0, 2),
+        (reduce_step, 0, 3, 1), (attend_some, 2), (reduce_step, 1, 0, 3), (reduce_step, 1, 3, 2),
+        (reduce_step, 0, 1, 2), (reduce_step, 0, 2, 2), (attend_some, 2), (reduce_step, 1, 1, 3),
+        (reduce_step, 1, 2, 3), (reduce_step, 0, 0, 3), (reduce_step, 0, 3, 2), (attend_some, 2),
+        (reduce_step, 1, 3, 3), (reduce_step, 0, 1, 3), (reduce_step, 0, 2, 3), (attend_some, 1), (activate, 0),
+        (reduce_step, 0, 3, 3), (activate, 1), (activate, 2), (attend_some, 1), (activate, 3), (attend_some, 1),
+        (forward, 0, 0, 1), (forward, 0, 1, 1), (forward, 0, 2, 1), (forward, 0, 3, 1), (attend_some, 2),
+        (forward, 0, 0, 2), (forward, 0, 1, 2), (forward, 0, 2, 2), (forward, 0, 3, 2), (spread_out, 1, 0),
+        (spread_out, 1, 1), (spread_out, 1, 2), (spread_out, 1, 3), (attend_some, 2), (forward, 0, 0, 3),
+        (forward, 0, 1, 3), (forward, 0, 2, 3), (forward, 0, 3, 3), (attend_some, 1), (forward, 1, 0, 1),
+        (forward, 1, 1, 1), (forward, 1, 2, 1), (forward, 1, 3, 1), (input_gradient, 0), (input_gradient, 1),
+        (input_gradient, 2), (input_gradient, 3), (attend_some, 1), (give_back, 0), (give_back, 1),
+        (give_back, 2), (give_back, 3), (weight_gradient, 0, 0), (weight_gradient, 0, 1), (weight_gradient, 0, 2),
+        (weight_gradient, 0, 3), (forward, 1, 0, 2), (forward, 1, 1, 2), (forward, 1, 2, 2), (forward, 1, 3, 2),
+        (attend_some, 1), (sum_y,), (hand_over, 0), (forward, 1, 0, 3), (forward, 1, 1, 3), (forward, 1, 2, 3),
+        (forward, 1, 3, 3), (sum_x,), (whole, 1, 0), (weight_gradient, 1, 0), (whole, 1, 1),
+        (weight_gradient, 1, 1), (whole, 1, 2), (weight_gradient, 1, 2), (whole, 1, 3), (weight_gradient, 1, 3),
+        (hand_over, 1),
     ]
     for step, *which in plan:
         step(*which)
@@ -490,7 +492,7 @@
         out_specs=(vmem,) * 3 + (hbm,) * 2,
         scratch_shapes=[
             vm(rows, BF16), vm(rows, BF16), vm(rows, BF16), vm(rows, BF16), vm(rows, BF16),
-            vm((2, 256, 512), BF16), vm((2, 256, 512), BF16), vm((128, 128), BF16),
+            vm((2, 256, 512), BF16), vm((2, 256, 512), BF16), vm((2, 256, 512), BF16), vm((128, 128), BF16),
             vm((8, D), F32), vm((8, D), F32), vm((8, D), F32), vm((512, 128), F32),
             vm((2, 8, 16, 256), BF16), vm((2, 8, 16, 256), BF16), vm((2, 4, 2, 4, 2, 32, 256), BF16),
             vm((2, 4, 8, 32, 512), BF16), vm((2, 2, 4, 4, 32, 512), BF16),
@@ -499,7 +501,7 @@
             vm((4, 2, 128, 512), BF16), vm((4, 128, 512), BF16), vm((4, 128, 512), BF16), vm((3, 128, 512), BF16),
             vm((4, 32, 512), BF16), vm((3, 32, 512), BF16), vm((8, 16, 256), BF16), vm((8, 16, 256), BF16),
             vm(rows, F32), vm(rows, F32),
-            dma((7,)), dma((2,)), dma((2, 4)), dma((2, 4)), dma((2, 7)), dma((2, 7)), dma((2, 3)), dma((2, 3)),
+            dma((9,)), dma((2,)), dma((2, 4)), dma((2, 4)), dma((2, 7)), dma((2, 7)), dma((2, 3)), dma((2, 3)),
             dma((2, 4)), dma((2, 4)), dma((2, 4)), dma((2, 4)),
             dma((2, 2, 4, 4)), dma((2, 2, 4, 4)), dma((2, 4, 8)), dma((2, 4, 8)), dma((4,)), dma((4,)), dma((3,)), dma((3,)),
             dma((3,)), dma((3,)), dma((7,)), dma((7,)), dma((2,)), dma((2,)),

time: 103 us -> 100 us (0.971)
  Pallas kernels: 102 us -> 99.3 us
    pallas_call x1, Pallas kernels: 97.7 us -> 95.1 us  [local(): pl.pallas_call(kernel, out_shape=(jax.ShapeDtypeStruct(rows, BF16), jax.S...]
where the time goes in v3:
time: 100 us
  Pallas kernels  99.3 us (99%)
    pallas_call x1, Pallas kernels, local(): pl.pallas_call(kernel, out_shape=(jax.ShapeDtypeStruct(rows, BF16), jax.S...  95.1 us
    pallas_call x1, Pallas kernels, local(): pl.pallas_call(write_out, out_shape=tuple((jax.ShapeDtypeStruct(part.shap...  4.19 us

profile of v3, /device:TPU:2, one launch (start us, length us, event | category | flops | bytes accessed | tf_op | source)
XLA Modules:
  0.0 100.1 jit_solution(12739256682857378551)
XLA Ops:
  0.6 95.1 %shard_map.128 = (bf16[128,4096]{1,0:T(8,128)(2,1)}, bf16[128,4096]{1,0:T(8,128)(2,1)}, bf16[128,4096]{1,0:T(8,128)(2,1)}, bf16[256,1024]{1,0:T(8,128)(2,1)}, bf16[256,1024]{1,0:T(8,128)(2,1)}) custom-call(s32[2,128]{1,0:T(2,128)} %bitcast.2, f32[2,128]{1,0:T(2,128)} %bitcast.3, bf16[128,4096]{1,0:T(8,128)(2,1)} %q_hbm.1, bf16[128,4096]{1,0:T(8,128)(2,1)} %k_hbm.1, ...), custom_call_target="tpu_custom_call" | custom-call | tf_op jit(solution)/shard_map/pallas_call | solution.py:482
  95.7 4.2 %shard_map.129 = (bf16[128,4096]{1,0:T(8,128)(2,1)}, bf16[128,4096]{1,0:T(8,128)(2,1)}, bf16[128,4096]{1,0:T(8,128)(2,1)}, bf16[256,1024]{1,0:T(8,128)(2,1)}, bf16[256,1024]{1,0:T(8,128)(2,1)}) custom-call(bf16[128,4096]{1,0:T(8,128)(2,1)} %get-tuple-element.10.refs_0_, bf16[128,4096]{1,0:T(8,128)(2,1)} %get-tuple-element.11.refs_1_, ...), custom_call_target="tpu_custom_call" | custom-call | tf_op jit(solution)/shard_map/pallas_call | solution.py:513

commit v4 on v3

--- a/solution.py
+++ b/solution.py
@@ -464,11 +464,22 @@
 
 
 def write_out(*refs):
-    sems = refs[10]
-    copies = [pltpu.make_async_copy(refs[n], refs[5 + n], sems.at[n]) for n in range(5)]
-    for copy in copies:
+    sources, results, held = refs[0:5], refs[5:10], refs[10:15]
+    read_sem, write_sem = refs[15:17]
+    reads, writes = [], []
+    for n in range(5):
+        half = sources[n].shape[0] // 2
+        for part_n in range(2):
+            rows = slice(part_n * half, part_n * half + half)
+            kept = held[n].at[rows]
+            reads.append(pltpu.make_async_copy(sources[n].at[rows], kept, read_sem.at[n, part_n]))
+            writes.append(pltpu.make_async_copy(kept, results[n].at[rows], write_sem.at[n, part_n]))
+    for copy in reads:
         copy.start()
-    for copy in copies:
+    for read, write in zip(reads, writes):
+        read.wait()
+        write.start()
+    for copy in writes:
         copy.wait()
 
 
@@ -513,9 +524,9 @@
     return pl.pallas_call(
         write_out,
         out_shape=tuple(jax.ShapeDtypeStruct(part.shape, part.dtype) for part in results),
-        in_specs=[vmem] * 5,
+        in_specs=[hbm] * 5,
         out_specs=(hbm,) * 5,
-        scratch_shapes=[dma((5,))],
+        scratch_shapes=[vm(part.shape, part.dtype) for part in results] + [dma((5, 2)), dma((5, 2))],
     )(*results)
 
 

time: 100 us -> 99.5 us (level)
  no operation moved by 1% of the time
where the time goes in v4:
time: 99.5 us; the launch traced here: 99.4 us
  Pallas kernels  98.6 us (99%)
    pallas_call x1, Pallas kernels, local(): pl.pallas_call(kernel, out_shape=(jax.ShapeDtypeStruct(rows, BF16), jax.S...  95.1 us
    pallas_call x1, Pallas kernels, local(): pl.pallas_call(write_out, out_shape=tuple((jax.ShapeDtypeStruct(part.shap...  3.51 us

profile of v4, /device:TPU:2, one launch (start us, length us, event | category | flops | bytes accessed | tf_op | source)
XLA Modules:
  0.0 99.4 jit_solution(14680160909432622048)
XLA Ops:
  0.6 95.1 %shard_map.128 = (bf16[128,4096]{1,0:T(8,128)(2,1)}, bf16[128,4096]{1,0:T(8,128)(2,1)}, bf16[128,4096]{1,0:T(8,128)(2,1)}, bf16[256,1024]{1,0:T(8,128)(2,1)}, bf16[256,1024]{1,0:T(8,128)(2,1)}) custom-call(s32[2,128]{1,0:T(2,128)} %bitcast.2, f32[2,128]{1,0:T(2,128)} %bitcast.3, bf16[128,4096]{1,0:T(8,128)(2,1)} %q_hbm.1, bf16[128,4096]{1,0:T(8,128)(2,1)} %k_hbm.1, ...), custom_call_target="tpu_custom_call" | custom-call | tf_op jit(solution)/shard_map/pallas_call | solution.py:493
  95.7 3.5 %shard_map.129 = (bf16[128,4096]{1,0:T(8,128)(2,1)}, bf16[128,4096]{1,0:T(8,128)(2,1)}, bf16[128,4096]{1,0:T(8,128)(2,1)}, bf16[256,1024]{1,0:T(8,128)(2,1)}, bf16[256,1024]{1,0:T(8,128)(2,1)}) custom-call(bf16[128,4096]{1,0:T(8,128)(2,1)} %get-tuple-element.10.refs_0_, bf16[128,4096]{1,0:T(8,128)(2,1)} %get-tuple-element.11.refs_1_, ...), custom_call_target="tpu_custom_call" | custom-call | tf_op jit(solution)/shard_map/pallas_call | solution.py:524
